TPU v7x, 512 devices: a whole 4x4x16 slice. The times are simulated.
512 devices in a mesh: blk: 128 (over y, z, core), face: 4 (over x).
Axes of the slice: x: 4, y: 4, z: 16, core: 2. Of those that a mesh axis runs over, the one named last changes fastest.
Arguments:
- flow_state: float32 [6, 16, 512, 1024], P(None, None, 'blk', 'face'), may hold values from -6 to 6
- viscosity: float32 [16, 512, 1024], P(None, 'blk', 'face'), may hold values from 0.03 to 0.15
- flux_jacobians: float32 [3, 6, 6], replicated, may hold values from -0.9 to 0.9
- rbf_weights: float32 [8, 24, 65536], P(None, None, ('blk', 'face')), may hold values from -1.25 to 1.25
- rbf_columns: int32 [4, 65536], P(None, ('blk', 'face')), may hold values from 0 to 255
- patch_owner: int32 [65536, 1], P(('blk', 'face')), may hold values from 0 to 127; in each aligned block of 128 rows (0 to 127, 128 to 255, ...) at most 8 rows name the same one
- stiff_blocks: float32 [8, 6, 6, 32768], P(None, None, None, 'blk'), as said below
- stiff_columns: int32 [8, 32768], P(None, 'blk'), may hold values from 0 to 511, as said below
Outputs:
- flow_out: float32 [6, 16, 512, 1024], P(None, None, 'blk', 'face')
- shell_motion: float32 [6, 32768], P(None, 'blk')
- surface_motion: float32 [8, 65536], P(None, ('blk', 'face'))
Inputs may be any that keep to these rules, and one draw needn't show every extreme that they name: `patch_owner`: among the patches of one device no owner is named more than 8 times, a bound that some block reaches. `stiff_columns`: block 0 and block 7 of node m point to m itself, block 7 being zero; the others come in pairs at node offsets +s and -s, one pair with s = 128, the same offsets for every node; K is symmetric and positive definite. `stiff_blocks`: K is symmetric and positive definite.
All inputs are finite; a program needn't handle non-finite values.
Results may differ from a plain program's by a relative error of at most 0.0003.
Values sent between devices are 32-bit elements; how exact they have to be, the bound alone decides.
A program may use at most 64 MiB of HBM per device.

v0:
```python
import jax
import jax.numpy as jnp
from jax import lax
from jax.sharding import PartitionSpec as P

DOF = 6
HB = 128
ITERS_CFD = 2
CG_ITERS = 4


HIGH = lax.Precision.HIGHEST


def with_halo(cells, sides, width):
    for axis, dim in sides:
        count = lax.axis_size(axis)
        ends = count - 1
        head = lax.slice_in_dim(cells, 0, width, axis=dim)
        tail = lax.slice_in_dim(cells, cells.shape[dim] - width, cells.shape[dim], axis=dim)
        cells = jnp.concatenate(
            [
                lax.ppermute(tail, axis, [(i, (i + 1) % count) for i in range(ends)]),
                cells,
                lax.ppermute(head, axis, [((i + 1) % count, i) for i in range(ends)]),
            ],
            axis=dim,
        )
    return cells


def relaxation(padded, viscosity, flux_jacobians):
    centre = padded[:, 1:-1, 1:-1, 1:-1]
    neighbours = (
        (padded[:, 2:, 1:-1, 1:-1], padded[:, :-2, 1:-1, 1:-1]),
        (padded[:, 1:-1, 2:, 1:-1], padded[:, 1:-1, :-2, 1:-1]),
        (padded[:, 1:-1, 1:-1, 2:], padded[:, 1:-1, 1:-1, :-2]),
    )
    spread = -6.0 * centre
    transport = jnp.zeros_like(centre)
    for axis_id in range(3):
        higher_side, lower_side = neighbours[axis_id]
        spread = spread + higher_side + lower_side
        transport = transport + jnp.einsum(
            "ij,jabc->iabc",
            flux_jacobians[axis_id],
            0.5 * (higher_side - lower_side),
            precision=HIGH,
        )
    return centre - transport + viscosity[None] * spread


def normal_pad(field):
    return jnp.pad(field, ((0, 0), (1, 1), (0, 0), (0, 0)))


def squared_total(vector):
    return lax.psum(jnp.sum(vector * vector), "blk")


def curvature_total(first_vec, second_vec):
    return lax.psum(jnp.sum(first_vec * second_vec), "blk")


def local(
    flow_state,
    viscosity,
    flux_jacobians,
    rbf_weights,
    rbf_columns,
    patch_owner,
    stiff_blocks,
    stiff_columns,
):
    state = flow_state
    span_count = viscosity.shape[1]
    chord_count = viscosity.shape[2]
    for sweep_index in range(ITERS_CFD):
        widened = with_halo(state, (("blk", 2), ("face", 3)), 1)
        state = relaxation(normal_pad(widened), viscosity, flux_jacobians)
    points = rbf_weights.shape[0]
    patches_here = span_count * (chord_count // points)
    wall = state[0, 0]
    pressure = (
        wall.reshape(span_count, chord_count // points, points)
        .transpose(2, 0, 1)
        .reshape(points, patches_here)
    )
    loads = jnp.einsum("pkn,pn->kn", rbf_weights, pressure, precision=HIGH)
    owners = lax.axis_size("blk")
    capacity = max(8, 2 * patches_here // owners)
    owner_of = patch_owner[:, 0]
    member_table = (owner_of[:, None] == jnp.arange(owners)[None, :]).astype(jnp.float32)
    earlier = (jnp.arange(patches_here)[:, None] > jnp.arange(patches_here)[None, :]).astype(
        jnp.float32
    )
    ahead = jnp.dot(earlier, member_table, precision=HIGH)
    rank_within = jnp.sum(ahead * member_table, axis=1)
    slot_of = owner_of.astype(jnp.float32) * capacity + rank_within
    packing = (
        slot_of[:, None] == jnp.arange(owners * capacity, dtype=jnp.float32)[None, :]
    ).astype(jnp.float32)
    sent_loads = jnp.dot(loads, packing, precision=HIGH)
    sent_nodes = jnp.dot((rbf_columns + 1).astype(jnp.float32), packing, precision=HIGH).astype(
        jnp.int32
    )
    got_loads, got_nodes = (
        lax.all_to_all(sent_loads, "blk", split_axis=1, concat_axis=1, tiled=True),
        lax.all_to_all(sent_nodes, "blk", split_axis=1, concat_axis=1, tiled=True),
    )
    node_count = stiff_blocks.shape[3]
    couplings = rbf_columns.shape[0]
    node_range = jnp.arange(node_count)
    tables = []
    assembled = jnp.zeros((DOF, node_count), jnp.float32)
    for member in range(couplings):
        table = ((got_nodes[member] - 1)[:, None] == node_range[None, :]).astype(jnp.float32)
        tables.append(table)
        assembled = assembled + jnp.dot(
            got_loads[member * DOF : (member + 1) * DOF], table, precision=HIGH
        )
    force = lax.psum(assembled, "face")
    solution = jnp.zeros_like(force)
    residual = force
    direction = force
    norm_now = squared_total(residual)
    for sweep_index in range(CG_ITERS):
        rimmed = with_halo(direction, (("blk", 1),), HB)
        taken = rimmed[:, stiff_columns]
        image = jnp.einsum("jcdn,djn->cn", stiff_blocks, taken, precision=HIGH)
        alpha = norm_now / curvature_total(direction, image)
        solution = solution + alpha * direction
        residual = residual - alpha * image
        norm_next = squared_total(residual)
        direction = residual + norm_next / norm_now * direction
        norm_now = norm_next
    replies = jnp.concatenate(
        [jnp.dot(solution, table.T, precision=HIGH) for table in tables], axis=0
    )
    returned = lax.all_to_all(replies, "blk", split_axis=1, concat_axis=1, tiled=True)
    node_values = jnp.dot(returned, packing.T, precision=HIGH)
    motion = jnp.einsum("pkn,kn->pn", rbf_weights, node_values, precision=HIGH)
    return (state, solution, motion)


def solution(mesh):
    placed = (
        P(None, None, "blk", "face"),
        P(None, "blk", "face"),
        P(),
        P(None, None, ("blk", "face")),
        P(None, ("blk", "face")),
        P(("blk", "face"), None),
        P(None, None, None, "blk"),
        P(None, "blk"),
    )
    return jax.shard_map(
        local,
        mesh=mesh,
        in_specs=placed,
        out_specs=(P(None, None, "blk", "face"), P(None, "blk"), P(None, ("blk", "face"))),
        check_vma=False,
    )
```

profile of v0, /device:TPU:1, one launch (start us, length us, event | category | flops | bytes accessed | tf_op | source)
XLA Modules:
  0.0 1957.4 jit_solution(9666418220128130672)
XLA Ops:
  2.0 4.9 collective-permute-start
  6.9 5.1 collective-permute-start.1
  13.4 3.1 collective-permute-start.2
  18.5 5.5 collective-permute-done.2
  24.0 4.1 collective-permute-done.3
  30.8 3.5 collective-permute-start.4
  37.7 21.4 %all-to-all-start.1 = ((s32[4,128,8]{2,0,1:T(4,128)}), s32[4,128,8]{2,0,1:T(4,128)S(1)}, u32[]{:S(2)}, u32[]{:S(2)}) async-start(s32[4,128,8]{2,0,1:T(4,128)} %copy.50), calls=%async_computation.1 | async-start | bytes 524288 | tf_op jit(solution)/shard_map/all_to_all | solution.py:109
  59.6 3.1 collective-permute-start.6
  64.8 5.4 collective-permute-done.6
  70.2 3.8 collective-permute-done.7
  81.6 16.4 all-to-all-start
  99.1 16.2 all-to-all-done
  120.3 7.0 psum.63
  127.3 5.9 collective-permute-start.8
  135.2 3.0 collective-permute-done.9
  138.3 5.5 gather_fusion
  144.7 244.9 %all-reduce.2 = (f32[]{:T(128)}, f32[]{:T(128)}) all-reduce(f32[]{:T(128)} %get-tuple-element.17, f32[]{:T(128)} %get-tuple-element.16), channel_id=1, replica_groups=mesh['blk'=128,'face'=4] {'blk'}, use_global_device_ids=true, to_apply=%region_3.4 | all-reduce | flops 2 | bytes 16 | tf_op jit(solution)/shard_map/psum | solution.py:58
  391.6 249.8 %psum.66 = f32[]{:T(128)} all-reduce(f32[]{:T(128)} %multiply_reduce_fusion.7), channel_id=1, replica_groups=mesh['blk'=128,'face'=4] {'blk'}, use_global_device_ids=true, to_apply=%region_7.8 | all-reduce | flops 1 | bytes 8 | tf_op jit(solution)/shard_map/psum | solution.py:58
  644.7 2.6 collective-permute-start.11
  649.8 5.5 gather_fusion.1
  656.2 245.4 %psum.67 = f32[]{:T(128)} all-reduce(f32[]{:T(128)} %fusion.60), channel_id=1, replica_groups=mesh['blk'=128,'face'=4] {'blk'}, use_global_device_ids=true, to_apply=%region_9.10 | all-reduce | flops 1 | bytes 8 | tf_op jit(solution)/shard_map/psum | solution.py:62
  903.6 249.3 %psum.68 = f32[]{:T(128)} all-reduce(f32[]{:T(128)} %get-tuple-element.20), channel_id=1, replica_groups=mesh['blk'=128,'face'=4] {'blk'}, use_global_device_ids=true, to_apply=%region_11.12 | all-reduce | flops 1 | bytes 8 | tf_op jit(solution)/shard_map/psum | solution.py:58
  1156.2 2.4 collective-permute-start.13
  1158.6 2.5 collective-permute-done.13
  1161.3 5.5 gather_fusion.2
  1167.7 245.4 %psum.69 = f32[]{:T(128)} all-reduce(f32[]{:T(128)} %fusion.58), channel_id=1, replica_groups=mesh['blk'=128,'face'=4] {'blk'}, use_global_device_ids=true, to_apply=%region_13.14 | all-reduce | flops 1 | bytes 8 | tf_op jit(solution)/shard_map/psum | solution.py:62
  1415.1 249.3 %psum.70 = f32[]{:T(128)} all-reduce(f32[]{:T(128)} %multiply_reduce_fusion.5), channel_id=1, replica_groups=mesh['blk'=128,'face'=4] {'blk'}, use_global_device_ids=true, to_apply=%region_15.16 | all-reduce | flops 1 | bytes 8 | tf_op jit(solution)/shard_map/psum | solution.py:58
  1670.1 2.5 collective-permute-done.15
  1672.7 5.5 gather_fusion.3
  1679.2 245.4 %psum.71 = f32[]{:T(128)} all-reduce(f32[]{:T(128)} %fusion.57), channel_id=1, replica_groups=mesh['blk'=128,'face'=4] {'blk'}, use_global_device_ids=true, to_apply=%region_17.18 | all-reduce | flops 1 | bytes 8 | tf_op jit(solution)/shard_map/psum | solution.py:62
  1929.8 7.7 all-to-all-start.2
  1938.4 16.6 all-to-all-done.2
  (123 shorter events, 52.5 us)
Async XLA Ops:
  0.6 11.7 copy-start.1
  0.6 11.4 copy-start.8
  2.0 10.3 collective-permute-start
  6.9 6.3 collective-permute-start.1
  12.3 5.5 copy-start.4
  13.4 10.6 collective-permute-start.2
  16.5 11.6 collective-permute-start.3
  18.5 10.9 copy-start.3
  29.4 6.9 copy-start.7
  30.8 28.2 %copy-start.2 = (f32[8,24,128]{2,1,0:T(8,128)S(1)}, f32[8,24,128]{2,1,0:T(8,128)}, u32[]{:S(2)}) copy-start(f32[8,24,128]{2,1,0:T(8,128)} %param.11) | copy-start | bytes 294916
  30.8 28.5 %collective-permute-start.4 = (f32[6,16,1,256]{3,0,2,1:T(8,128)S(1)}, f32[6,16,1,256]{3,0,2,1:T(8,128)S(1)}, u32[]{:S(2)}, u32[]{:S(2)}) collective-permute-start(f32[6,16,1,256]{3,0,2,1:T(8,128)S(1)} %get-tuple-element.26), channel_id=1, source_target_pairs={{0,4},{4,8},{8,12},{12,16},{16,20},{20,24},{24,28},{28,32},{32,36}... | collective-permute-start | bytes 294920 | tf_op jit(solution)/shard_map/ppermute | solution.py:23
  34.3 25.0 %collective-permute-start.5 = (f32[6,16,1,256]{3,0,2,1:T(8,128)S(1)}, f32[6,16,1,256]{3,0,2,1:T(8,128)S(1)}, u32[]{:S(2)}, u32[]{:S(2)}) collective-permute-start(f32[6,16,1,256]{3,0,2,1:T(8,128)S(1)} %get-tuple-element.27), channel_id=1, source_target_pairs={{4,0},{8,4},{12,8},{16,12},{20,16},{24,20},{28,24},{32,28},{36,32}... | collective-permute-start | bytes 294920 | tf_op jit(solution)/shard_map/ppermute | solution.py:25
  37.7 43.9 %all-to-all-start.1 = ((s32[4,128,8]{2,0,1:T(4,128)}), s32[4,128,8]{2,0,1:T(4,128)S(1)}, u32[]{:S(2)}, u32[]{:S(2)}) async-start(s32[4,128,8]{2,0,1:T(4,128)} %copy.50), calls=%async_computation.1 | async-start | bytes 524288 | tf_op jit(solution)/shard_map/all_to_all | solution.py:109
  59.6 10.6 collective-permute-start.6
  62.7 11.3 collective-permute-start.7
  77.2 20.7 %copy-start.5 = (s32[8,256]{1,0:T(8,128)S(1)}, s32[8,256]{1,0:T(8,128)}, u32[]{:S(2)}) copy-start(s32[8,256]{1,0:T(8,128)} %param.15) | copy-start | bytes 24580
  81.6 33.8 %all-to-all-start = ((f32[128,1,192]{2,1,0:T(1,128)}), f32[128,1,192]{2,1,0:T(1,128)S(1)}, u32[]{:S(2)}, u32[]{:S(2)}) async-start(f32[128,1,192]{2,1,0:T(1,128)} %reshape.136), calls=%async_computation | async-start | bytes 262144 | tf_op jit(solution)/shard_map/all_to_all | solution.py:108
  119.5 24.6 %copy-start = (f32[8,6,6,256]{3,0,2,1:T(8,128)S(1)}, f32[8,6,6,256]{3,0,2,1:T(8,128)}, u32[]{:S(2)}) copy-start(f32[8,6,6,256]{3,0,2,1:T(8,128)} %param.14) | copy-start | bytes 884740
  127.3 7.8 collective-permute-start.8
  133.2 4.9 collective-permute-start.9
  642.8 4.6 collective-permute-start.10
  644.7 4.9 collective-permute-start.11
  1154.2 4.3 collective-permute-start.12
  1156.2 4.9 collective-permute-start.13
  1665.7 4.3 collective-permute-start.14
  1667.7 4.9 collective-permute-start.15
  1926.0 2.8 copy-start.6
  1929.8 25.2 %all-to-all-start.2 = ((f32[128,1,192]{2,1,0:T(1,128)}), f32[128,1,192]{2,1,0:T(1,128)S(1)}, u32[]{:S(2)}, u32[]{:S(2)}) async-start(f32[128,1,192]{2,1,0:T(1,128)} %reshape.138), calls=%async_computation.2 | async-start | bytes 262144 | tf_op jit(solution)/shard_map/all_to_all | solution.py:140
where the time goes:
time: 1960 us
  blocking collectives  1740 us (89%)
  starting transfers between devices  90.9 us (5%)
  waiting for transfers between devices  64.2 us (3%)
  local copies, waits for them, and re-layouts  31.6 us (2%)
    psum x4, blocking collectives, squared_total(): return lax.psum(jnp.sum(vector * vector), 'blk')  993 us
    psum x3, blocking collectives, curvature_total(): return lax.psum(jnp.sum(first_vec * second_vec), 'blk')  736 us
  transfers between devices with their start and end apart: 19, of which 12 were waited for; matrix products, arithmetic and copies ran while one was open for 1% of the time, Pallas kernels for 0%

commit v1 on v0

v1 whole, which is shorter than its diff:
```python
import functools

import jax
import jax.numpy as jnp
from jax import lax
from jax.experimental import pallas as pl
from jax.experimental.pallas import tpu as pltpu
from jax.sharding import PartitionSpec as P

MESH = pl.DeviceIdType.MESH
F32 = jnp.float32
BF16 = jnp.bfloat16
DOF = 6
WALL = 3
CORES = 2
REACH = 2


def iota(shape, dim):
    return lax.broadcasted_iota(jnp.int32, shape, dim)


def three_parts(x):
    high = x.astype(BF16).astype(F32)
    rest = x - high
    middle = rest.astype(BF16).astype(F32)
    return high, middle, rest - middle


def stacked_parts(x):
    return jnp.concatenate(three_parts(x), axis=0)


def exact_dot(x, table, dims):
    rows = x.shape[0]
    out = lax.dot_general(
        stacked_parts(x).astype(BF16), table, (dims, ((), ())), preferred_element_type=F32
    )
    return out[:rows] + out[rows : 2 * rows] + out[2 * rows :]


NN_DIMS = ((1,), (0,))
NT_DIMS = ((1,), (1,))


def kernel(
    ny, nz, nf,
    flow, visc, jac, rbf, cols, owner, kmat, kcols,
    out_flow, out_shell, out_motion,
    raw, left, right, q0, q1, q2, rbf_v, kw,
    pick, pack, nodes_out, nodes_in, one_hot, one_hot_t, loads_out, loads_in, lhs,
    part_out, part_in, force_out, force_in, dots1_a, dots1_b, dots2_a, dots2_b,
    ans_out, ans_in, vals_out, vals_in, ssem, rsem, lsem,
):
    nc = CORES
    ng = ny * nc
    nb = ny * nz * nc
    cap = 128 // nz
    b = lax.axis_index("blk")
    f = lax.axis_index("face")
    y = b // (nz * nc)
    z = (b // nc) % nz
    c = b % nc
    g = y * nc + c

    def near(ob, of):
        return ((b + ob + nb) % nb, (f + of + nf) % nf)

    def along_g(d):
        other = (g + d + ng) % ng
        return ((other // nc) * (nz * nc) + z * nc + other % nc, f)

    def along_z(d):
        return (y * (nz * nc) + ((z + d + nz) % nz) * nc + c, f)

    used = [0]

    def send(src, dst, to):
        i = used[0]
        used[0] += 1
        copy = pltpu.make_async_remote_copy(
            src_ref=src, dst_ref=dst, send_sem=ssem.at[i], recv_sem=rsem.at[i],
            device_id=to, device_id_type=MESH,
        )
        copy.start()
        sent.append(copy)
        return copy

    sent = []

    local_wall = [
        pltpu.make_async_copy(flow.at[:, 0:WALL], raw.at[0:6, 0:WALL, 2:6, :], lsem.at[0]),
        pltpu.make_async_copy(visc.at[0:WALL], raw.at[6, 0:WALL, 2:6, :], lsem.at[1]),
    ]
    nk = visc.shape[0]
    local_rest = [
        pltpu.make_async_copy(flow.at[:, WALL:nk], raw.at[0:6, WALL:nk, 2:6, :], lsem.at[2]),
        pltpu.make_async_copy(visc.at[WALL:nk], raw.at[6, WALL:nk, 2:6, :], lsem.at[3]),
    ]
    local_k = pltpu.make_async_copy(kmat, kw.at[REACH], lsem.at[4])
    local_rbf = pltpu.make_async_copy(rbf, rbf_v, lsem.at[5])
    for copy in local_wall:
        copy.start()
    local_rbf.start()
    for copy in local_rest:
        copy.start()
    local_k.start()

    around = [(ob, of) for of in range(nf) for ob in range(-REACH, REACH + 1) if (ob, of) != (0, 0)]
    peers = [near(ob, of) for ob, of in around]
    peers += [along_g(d) for d in range(1, ng)]
    peers += [along_z(d) for d in range(1, nz)]
    barrier = pltpu.get_barrier_semaphore()
    for peer in peers:
        pl.semaphore_signal(barrier, inc=1, device_id=peer, device_id_type=MESH)

    pick[...] = (iota((1024, 128), 1) == (iota((1024, 128), 0) // 256) * 32 + (iota((1024, 128), 0) % 256) // 8).astype(BF16)
    own = owner[...]
    members = (own == iota((128, nb if nb > 128 else 128), 1)).astype(F32)
    earlier = (iota((128, 128), 0) > iota((128, 128), 1)).astype(F32)
    ahead = jnp.dot(earlier.astype(BF16), members.astype(BF16), preferred_element_type=F32)
    rank = jnp.sum(ahead * members, axis=1, keepdims=True).astype(jnp.int32)
    own_c = own % nc
    own_z = (own // nc) % nz
    own_g = (own // (nz * nc)) * nc + own_c
    slot = own_z * cap + rank
    lane = iota((128, 128), 1)
    for d in range(ng):
        here = (own_g == (g + d) % ng) & (slot == lane)
        pack[:, d * 128 : (d + 1) * 128] = here.astype(F32).astype(BF16)
    named = (cols[...] + 1).astype(F32)
    named = jnp.concatenate([named, jnp.zeros((4, 128), F32)], axis=0)
    packed_nodes = lax.dot_general(
        named.astype(BF16), pack[...], (NN_DIMS, ((), ())), preferred_element_type=F32
    )
    for d in range(ng):
        nodes_out[d] = packed_nodes[:, d * 128 : (d + 1) * 128]

    pl.semaphore_wait(barrier, len(peers))
    for copy in local_wall:
        copy.wait()

    def halo(lo, hi):
        ks = pl.ds(lo, hi - lo)
        low, high = pl.ds(0, 128), pl.ds(128, 128)
        return [
            send(raw.at[:, ks, 4:6, :], raw.at[:, ks, 0:2, :], near(1, 0)),
            send(raw.at[:, ks, 2:4, :], raw.at[:, ks, 6:8, :], near(-1, 0)),
            send(raw.at[:, ks, 2:6, high], left.at[:, ks, 2:6, :], near(0, 1)),
            send(raw.at[:, ks, 2:6, low], right.at[:, ks, 2:6, :], near(0, -1)),
            send(raw.at[:, ks, 5:6, high], left.at[:, ks, 1:2, :], near(1, 1)),
            send(raw.at[:, ks, 5:6, low], right.at[:, ks, 1:2, :], near(1, -1)),
            send(raw.at[:, ks, 2:3, high], left.at[:, ks, 6:7, :], near(-1, 1)),
            send(raw.at[:, ks, 2:3, low], right.at[:, ks, 6:7, :], near(-1, -1)),
        ]

    wall_halo = halo(0, WALL)
    node_copies = [send(nodes_out.at[d], nodes_in.at[d], along_g(d)) for d in range(1, ng)]

    row8 = iota((8, 384), 0)
    lane384 = iota((8, 384), 1)
    inside = ((b > 0) | (row8 >= 2)) & ((b < nb - 1) | (row8 < 6))
    inside = inside & ((lane384 < 256) | ((row8 >= 1) & (row8 < 7)))
    inside = inside & ((f < nf - 1) | (lane384 < 256) | (lane384 >= 320))
    inside = inside & ((f > 0) | (lane384 < 320))
    from_right = iota((8, 128), 1) < 64

    zero_plane = jnp.zeros((8, 384), F32)
    for v in range(6):
        for buf in (q0, q1):
            buf[v, 0] = zero_plane
            buf[v, nk + 1] = zero_plane

    def clean(k):
        for v in range(7):
            edge = jnp.where(from_right, right[v, k], left[v, k])
            q0[v, k + 1] = jnp.where(inside, jnp.concatenate([raw[v, k], edge], axis=1), 0.0)

    def relax(src, k, wide, variables):
        diffs = []
        spreads = {}
        centres = {}
        for v in range(6):
            mid = src[v, k + 1]
            trio = [
                (src[v, k + 2, :, 0:wide], src[v, k, :, 0:wide]),
                (pltpu.roll(mid, 7, 0)[:, 0:wide], pltpu.roll(mid, 1, 0)[:, 0:wide]),
                (pltpu.roll(mid, 383, 1)[:, 0:wide], pltpu.roll(mid, 1, 1)[:, 0:wide]),
            ]
            diffs.append([0.5 * (hi - lo) for hi, lo in trio])
            if v in variables:
                centres[v] = mid[:, 0:wide]
                total = -6.0 * centres[v]
                for hi, lo in trio:
                    total = total + hi + lo
                spreads[v] = total
        visc_here = q0[6, k + 1, :, 0:wide]
        result = []
        for i in variables:
            moved = None
            for d in range(3):
                for v in range(6):
                    term = jac[(d * 6 + i) * 6 + v] * diffs[v][d]
                    moved = term if moved is None else moved + term
            result.append(centres[i] - moved + visc_here * spreads[i])
        return result

    def first_sweep(k):
        for v, val in enumerate(relax(q0, k, 384, range(6))):
            q1[v, k + 1] = jnp.where(inside, val, 0.0)

    for copy in wall_halo:
        copy.wait_recv()
    for k in range(WALL):
        clean(k)
    for k in range(WALL - 1):
        first_sweep(k)
    wall = relax(q1, 0, 256, [0])[0]
    of_point = iota((8, 256), 1) % 8 == iota((8, 256), 0)
    spread_wall = jnp.concatenate(
        [jnp.where(of_point, jnp.broadcast_to(wall[2 + i : 3 + i], (8, 256)), 0.0) for i in range(4)],
        axis=1,
    )
    pressure = exact_dot(spread_wall, pick[...], NN_DIMS)
    local_rbf.wait()
    loads = None
    for p in range(8):
        term = rbf_v[p] * pressure[p : p + 1]
        loads = term if loads is None else loads + term
    gap = jnp.zeros((2, 128), F32)
    tall = []
    for k in range(4):
        tall += [loads[k * 6 : k * 6 + 6], gap]
    packed = exact_dot(jnp.concatenate(tall, axis=0), pack[...], NN_DIMS)
    for d in range(ng):
        loads_out[d] = packed[:, d * 128 : (d + 1) * 128]
    load_copies = [send(loads_out.at[d], loads_in.at[d], along_g(d)) for d in range(1, ng)]

    for copy in local_rest:
        copy.wait()
    rest_halo = halo(WALL, nk)
    local_k.wait()
    k_copies = [send(kw.at[REACH], kw.at[REACH - o], near(o, 0)) for o in (1, -1, 2, -2)]

    nodes_in[0] = nodes_out[0]
    loads_in[0] = loads_out[0]
    for copy in node_copies:
        copy.wait_recv()
    lane256 = iota((128, 256), 1) + 1
    for d in range(ng):
        upright = jnp.transpose(
            jnp.concatenate([nodes_in[d], jnp.zeros((120, 128), F32)], axis=0)
        ).astype(jnp.int32)
        for k in range(4):
            hit = upright[:, k : k + 1] == lane256
            one_hot[(d * 4 + k) * 128 : (d * 4 + k + 1) * 128, :] = hit.astype(F32).astype(BF16)

    for copy in load_copies:
        copy.wait_recv()
    slot_z = iota((nz, 24, 128), 2) // cap
    dest_z = (iota((nz, 24, 128), 0) + z) % nz
    to_dest = slot_z == dest_z
    for d in range(ng):
        for k in range(4):
            parts = stacked_parts(loads_in[d, k * 8 : k * 8 + 8, :])
            masked = jnp.where(to_dest, jnp.broadcast_to(parts[None], (nz, 24, 128)), 0.0)
            at = (d * 4 + k) * 128
            lhs[:, at : at + 128] = masked.reshape(nz * 24, 128).astype(BF16)
    dense = jnp.dot(lhs[...], one_hot[...], preferred_element_type=F32)
    for d in range(nz):
        part = dense[d * 24 : d * 24 + 24]
        part_out[d] = part[0:8] + part[8:16] + part[16:24]
    part_copies = [
        send(part_out.at[d, 0:6, :], part_in.at[d, 0:6, :], along_z(d)) for d in range(1, nz)
    ]

    for copy in rest_halo:
        copy.wait_recv()

    def clean_loop(k, carry):
        clean(k)
        return carry

    def first_loop(k, carry):
        first_sweep(k)
        return carry

    lax.fori_loop(WALL, nk, clean_loop, 0)
    lax.fori_loop(WALL - 1, nk, first_loop, 0)

    total = part_out[0, 0:6, :]
    for d in range(1, nz):
        part_copies[d - 1].wait_recv()
        total = total + part_in[d, 0:6, :]
    force_out[...] = total
    force_copies = {}
    for ob, of in around:
        force_copies[ob, of] = send(force_out, force_in.at[of, ob + REACH], near(ob, of))

    for d in range(ng):
        for k in range(4):
            row = nodes_in[d, k : k + 1, :].astype(jnp.int32)
            hit = row == iota((256, 128), 0) + 1
            at = (d * 4 + k) * 128
            one_hot_t[:, at : at + 128] = hit.astype(F32).astype(BF16)

    def second_loop(k, carry):
        for v, val in enumerate(relax(q1, k, 256, range(6))):
            q2[v, k] = val
        return carry

    lax.fori_loop(0, nk, second_loop, 0)
    flow_copy = pltpu.make_async_copy(q2.at[:, :, 2:6, :], out_flow, lsem.at[6])
    flow_copy.start()

    for copy in force_copies.values():
        copy.wait_recv()
    for copy in k_copies:
        copy.wait_recv()

    def of_face(ob, df):
        return force_out[...] if (ob, df) == (0, 0) else force_in[df, ob + REACH]

    valid = [(b + p >= 0) & (b + p < nb) for p in range(-REACH, REACH + 1)]
    empty = jnp.zeros((2, 128), F32)
    start = []
    for p in range(-REACH, REACH + 1):
        terms = [of_face(-p, df) for df in range(nf)]
        if nf == 4:
            full = (terms[0] + terms[2]) + (terms[1] + terms[3])
        else:
            full = terms[0] + terms[1]
        full = jnp.where(valid[p + REACH], full, 0.0)
        for half in range(2):
            start.append(jnp.concatenate([full[:, half * 128 : half * 128 + 128], empty], axis=0))
    v0 = dict(enumerate(start))

    reach = [kcols[j, 0] for j in range(8)]
    lane128 = iota((8, 128), 1)

    def times_k(vec, lo, hi):
        shifted = {i: [vec[i]] for i in range(lo, hi)}
        for j in range(1, 7):
            rest = reach[j] % 128
            whole = reach[j] // 128
            back = (128 - rest) % 128
            turned = {i: pltpu.roll(vec[i], back, 1) for i in range(lo - 1, hi + 1)}
            stay = lane128 + rest < 128
            joined = {i: jnp.where(stay, turned[i], turned[i + 1]) for i in range(lo - 1, hi)}
            for i in range(lo, hi):
                far = jnp.where(whole == 1, joined[i], turned[i + 1])
                shifted[i].append(jnp.where(whole == 0, joined[i - 1], far))
        for i in range(lo, hi):
            shifted[i].append(vec[i])
        out = {}
        for i in range(lo, hi):
            lanes = pl.ds((i % 2) * 128, 128)
            rows = []
            for r in range(DOF):
                total = None
                for j in range(8):
                    term = kw[i // 2, j, r, :, lanes] * shifted[i][j][0:6]
                    total = term if total is None else total + term
                rows.append(jnp.sum(total, axis=0, keepdims=True))
            rows.append(empty)
            out[i] = jnp.where(valid[i // 2], jnp.concatenate(rows, axis=0), 0.0)
        return out

    mid = (2 * REACH, 2 * REACH + 1)

    def dot_row(one, two):
        return jnp.sum(sum(one[i] * two[i] for i in mid), axis=0, keepdims=True)

    def everywhere(rows, buf_a, buf_b):
        height = buf_a.shape[1]
        rows = rows + [jnp.zeros((height - len(rows), 128), F32)]
        buf_a[0] = jnp.concatenate(rows, axis=0)
        copies = [send(buf_a.at[0], buf_a.at[d], along_z(d)) for d in range(1, nz)]
        for copy in copies:
            copy.wait_recv()
        buf_b[0] = functools.reduce(jnp.add, [buf_a[d] for d in range(nz)])
        copies = [send(buf_b.at[0], buf_b.at[d], along_g(d)) for d in range(1, ng)]
        for copy in copies:
            copy.wait_recv()
        total = functools.reduce(jnp.add, [buf_b[d] for d in range(ng)])
        total = jnp.sum(total, axis=1, keepdims=True)
        return [total[i : i + 1] for i in range(len(rows) - 1)]

    def mix(scales_and_vecs, lo, hi):
        out = {}
        for i in range(lo, hi):
            total = None
            for scale, vec in scales_and_vecs:
                term = vec[i] if scale is None else scale * vec[i]
                total = term if total is None else total + term
            out[i] = total
        return out

    v1 = times_k(v0, 1, 9)
    v2 = times_k(v1, 2, 8)
    m0, m1, m2, m3 = everywhere(
        [dot_row(v0, v0), dot_row(v0, v1), dot_row(v1, v1), dot_row(v1, v2)], dots1_a, dots1_b
    )
    alpha0 = m0 / m1
    rr1 = jnp.maximum(m0 - 2.0 * alpha0 * m1 + alpha0 * alpha0 * m2, 0.0)
    beta0 = rr1 / m0
    bend1 = (m1 - 2.0 * alpha0 * m2 + alpha0 * alpha0 * m3) + 2.0 * beta0 * (m1 - alpha0 * m2) + beta0 * beta0 * m1
    alpha1 = rr1 / bend1
    r1 = mix([(None, v0), (-alpha0, v1)], 2, 8)
    d1 = mix([(None, r1), (beta0, v0)], 2, 8)
    t = mix([(1.0 + beta0, v1), (-alpha0, v2)], 2, 8)
    x2 = mix([(alpha0, v0), (alpha1, d1)], 4, 6)
    r2 = mix([(None, r1), (-alpha1, t)], 2, 8)
    s = times_k(r2, 3, 7)
    u = times_k(s, 4, 6)
    w = times_k(t, 4, 6)
    pairs = [(r2, r2), (r2, s), (r2, t), (d1, t), (s, s), (s, t), (t, t), (s, u), (s, w), (t, w)]
    rr2, rs, rt, dt, ss, st, tt, su, sw, tw = everywhere(
        [dot_row(one, two) for one, two in pairs], dots2_a, dots2_b
    )
    beta1 = rr2 / rr1
    bend2 = rs + 2.0 * beta1 * rt + beta1 * beta1 * dt
    alpha2 = rr2 / bend2
    along = rs + beta1 * rt
    square = ss + 2.0 * beta1 * st + beta1 * beta1 * tt
    rr3 = jnp.maximum(rr2 - 2.0 * alpha2 * along + alpha2 * alpha2 * square, 0.0)
    beta2 = rr3 / rr2
    bend3 = (
        rs
        - 2.0 * alpha2 * (ss + beta1 * st)
        + alpha2 * alpha2 * (su + 2.0 * beta1 * sw + beta1 * beta1 * tw)
        + 2.0 * beta2 * (along - alpha2 * square)
        + beta2 * beta2 * bend2
    )
    alpha3 = rr3 / bend3
    d2 = mix([(None, r2), (beta1, d1)], 4, 6)
    w2 = mix([(None, s), (beta1, t)], 4, 6)
    r3 = mix([(None, r2), (-alpha2, w2)], 4, 6)
    d3 = mix([(None, r3), (beta2, d2)], 4, 6)
    x4 = mix([(None, x2), (alpha2, d2), (alpha3, d3)], 4, 6)
    answer = jnp.concatenate([x4[4], x4[5]], axis=1)
    ans_out[...] = answer
    ans_copies = [
        send(ans_out.at[0:6, :], ans_in.at[d, 0:6, :], along_z(d)) for d in range(1, nz)
    ]
    out_shell[...] = answer[0:6]

    level = []
    zero2 = jnp.zeros((2, 256), F32)
    for d in range(nz):
        if d == 0:
            level.append(stacked_parts(answer))
        else:
            ans_copies[d - 1].wait_recv()
            level.append(stacked_parts(jnp.concatenate([ans_in[d, 0:6, :], zero2], axis=0)))
    wide_x = jnp.concatenate(level, axis=0).astype(BF16)
    from_z = (z + nz - iota((nz, 8, 256), 0)) % nz
    from_here = (iota((nz, 8, 256), 2) % 128) // cap == from_z
    for d in range(ng):
        for k in (0, 2):
            at = (d * 4 + k) * 128
            got = jnp.dot(wide_x, one_hot_t[:, at : at + 256], preferred_element_type=F32)
            got = got.reshape(nz, 3, 8, 256)
            got = got[:, 0] + got[:, 1] + got[:, 2]
            got = jnp.sum(jnp.where(from_here, got, 0.0), axis=0)
            vals_out[d, k * 8 : k * 8 + 8, :] = got[:, 0:128]
            vals_out[d, k * 8 + 8 : k * 8 + 16, :] = got[:, 128:256]
    val_copies = [send(vals_out.at[d], vals_in.at[d], along_g(-d)) for d in range(1, ng)]
    returned = [vals_out[0]]
    for d in range(1, ng):
        val_copies[d - 1].wait_recv()
        returned.append(vals_in[d])
    values = exact_dot(jnp.concatenate(returned, axis=1), pack[...], NT_DIMS)
    values = jnp.concatenate([values[k * 8 : k * 8 + 6] for k in range(4)], axis=0)
    motion = [jnp.sum(rbf_v[p] * values, axis=0, keepdims=True) for p in range(8)]
    out_motion[...] = jnp.concatenate(motion, axis=0)

    flow_copy.wait()
    for copy in sent:
        copy.wait_send()


def solution(mesh):
    nb, nf = mesh.shape["blk"], mesh.shape["face"]
    ny = 4 if nb == 128 else 2
    nz = nb // (ny * CORES)
    ng = ny * CORES
    count = 8 * 2 + 4 + (ng - 1) * 5 + (nz - 1) * 4 + (5 * nf - 1)

    def local(flow, visc, jac, rbf, cols, owner, kmat, kcols):
        nk = visc.shape[0]
        vmem = pl.BlockSpec(memory_space=pltpu.VMEM)
        smem = pl.BlockSpec(memory_space=pltpu.SMEM)
        hbm = pl.BlockSpec(memory_space=pl.ANY)
        k_total = ng * 512
        scratch = [
            ((7, nk, 8, 256), F32),
            ((7, nk, 8, 128), F32),
            ((7, nk, 8, 128), F32),
            ((7, nk + 2, 8, 384), F32),
            ((6, nk + 2, 8, 384), F32),
            ((6, nk, 8, 256), F32),
            ((8, 24, 128), F32),
            ((5, 8, 6, 6, 256), F32),
            ((1024, 128), BF16),
            ((128, ng * 128), BF16),
            ((ng, 8, 128), F32),
            ((ng, 8, 128), F32),
            ((k_total, 256), BF16),
            ((256, k_total), BF16),
            ((ng, 32, 128), F32),
            ((ng, 32, 128), F32),
            ((nz * 24, k_total), BF16),
            ((nz, 8, 256), F32),
            ((nz, 8, 256), F32),
            ((6, 256), F32),
            ((nf, 5, 6, 256), F32),
            ((nz, 8, 128), F32),
            ((ng, 8, 128), F32),
            ((nz, 16, 128), F32),
            ((ng, 16, 128), F32),
            ((8, 256), F32),
            ((nz, 8, 256), F32),
            ((ng, 32, 128), F32),
            ((ng, 32, 128), F32),
        ]
        return pl.pallas_call(
            functools.partial(kernel, ny, nz, nf),
            out_shape=(
                jax.ShapeDtypeStruct(flow.shape, F32),
                jax.ShapeDtypeStruct((6, 256), F32),
                jax.ShapeDtypeStruct((8, 128), F32),
            ),
            in_specs=[hbm, hbm, smem, hbm, vmem, vmem, hbm, smem],
            out_specs=(hbm, vmem, vmem),
            scratch_shapes=[pltpu.VMEM(shape, kind) for shape, kind in scratch]
            + [
                pltpu.SemaphoreType.DMA((count,)),
                pltpu.SemaphoreType.DMA((count,)),
                pltpu.SemaphoreType.DMA((8,)),
            ],
            compiler_params=pltpu.CompilerParams(
                collective_id=0, has_side_effects=True, vmem_limit_bytes=48 * 1024 * 1024
            ),
        )(flow, visc, jac.reshape(-1), rbf, cols, owner, kmat, kcols)

    placed = (
        P(None, None, "blk", "face"),
        P(None, "blk", "face"),
        P(),
        P(None, None, ("blk", "face")),
        P(None, ("blk", "face")),
        P(("blk", "face"), None),
        P(None, None, None, "blk"),
        P(None, "blk"),
    )
    return jax.shard_map(
        local,
        mesh=mesh,
        in_specs=placed,
        out_specs=(P(None, None, "blk", "face"), P(None, "blk"), P(None, ("blk", "face"))),
        check_vma=False,
    )
```

time: 1960 us -> 101 us (0.05)
  blocking collectives: 1740 us -> 0 us
  Pallas kernels: 0 us -> 96.3 us
  starting transfers between devices: 90.9 us -> 0 us
  waiting for transfers between devices: 64.2 us -> 0 us
  local copies, waits for them, and re-layouts: 31.6 us -> 4.06 us
    psum x8 -> x0, blocking collectives: 1740 us -> none  [the longest x4 993 us: squared_total(): return lax.psum(jnp.sum(vector * vector), 'blk')]
    pallas_call x0 -> x1, Pallas kernels: none -> 96.3 us  [local(): pl.pallas_call(functools.partial(kernel, ny, nz, nf), out_shape=(jax.Shap...]
    ppermute x16 -> x0, starting transfers between devices: 45.5 us -> none  [the longest x8 26.3 us: with_halo(): lax.ppermute(tail, axis, [(i, (i + 1) % count) for i in range(ends)])]
    all_to_all x3 -> x0, starting transfers between devices: 45.4 us -> none  [the longest x1 21.4 us: local(): lax.all_to_all(sent_nodes, 'blk', split_axis=1, concat_axis=1, tiled=True)]
    all_to_all x3 -> x0, waiting for transfers between devices: 34.4 us -> none  [the longest x1 16.6 us: local(): lax.all_to_all(replies, 'blk', split_axis=1, concat_axis=1, tiled=True)]
    ppermute x16 -> x0, waiting for transfers between devices: 29.7 us -> none  [the longest x8 18.9 us: with_halo(): lax.ppermute(head, axis, [((i + 1) % count, i) for i in range(ends)])]
    gather x4 -> x0, local copies, waits for them, and re-layouts: 21.8 us -> none  [local(): taken = rimmed[:, stiff_columns]]
  transfers between devices with their start and end apart: 19 -> 0, of which waited for: 12 -> 0; matrix products, arithmetic and copies ran while one was open for 1% -> 0% of each run, Pallas kernels for 0% -> 0%
where the time goes in v1:
time: 101 us
  Pallas kernels  96.3 us (95%)
  local copies, waits for them, and re-layouts  4.06 us (4%)
    pallas_call x1, Pallas kernels, local(): pl.pallas_call(functools.partial(kernel, ny, nz, nf), out_shape=(jax.Shap...  96.3 us
    unnamed x17, local copies, waits for them, and re-layouts  3.21 us

profile of v1, /device:TPU:1, one launch (start us, length us, event | category | flops | bytes accessed | tf_op | source)
XLA Modules:
  0.0 101.1 jit_solution(14555119635079666512)
XLA Ops:
  0.6 0.0 copy-start.5
  0.6 0.0 copy-start
  0.7 0.8 reshape.9.jac
  1.5 0.0 copy-done.5
  1.5 0.1 copy.11.owner
  1.6 0.0 copy-start.1
  1.6 0.0 copy-start.2
  1.6 0.0 copy-start.3
  1.6 0.0 copy-start.4
  1.7 1.1 %copy.12.kmat = f32[8,6,6,256]{3,2,1,0:T(8,128)S(1)} copy(f32[8,6,6,256]{3,0,2,1:T(8,128)} %param.14) | data formatting | bytes 589824 | tf_op args[6]
  2.8 0.0 copy-done
  2.8 0.0 copy-done.1
  2.8 0.0 copy-done.2
  2.8 0.0 copy-done.3
  2.8 0.0 copy-done.4
  2.8 96.3 %shard_map.103 = (f32[6,16,4,256]{3,2,1,0:T(4,128)S(1)}, f32[6,256]{1,0:T(8,128)S(1)}, f32[8,128]{1,0:T(8,128)S(1)}) custom-call(f32[6,16,4,256]{3,2,1,0:T(4,128)S(1)} %copy-done, f32[16,4,256]{2,1,0:T(4,128)S(1)} %copy-done.2, f32[108]{0:T(128)S(1)} %reshape.9.jac, f32[8,24,128]{2,1,0:T(8,128)S(1)} %copy-done.1, s32[4,128]{1,0:T(4,128)S(1)} %copy-done.4, ...), custom_call_target="tpu_custom_call" | custom-call | tf_op jit(solution)/shard_map/pallas_call | solution.py:527
  99.2 0.7 copy.16
  100.0 0.6 copy.17
  100.6 0.6 copy.18
Async XLA Ops:
  0.6 0.9 copy-start.5
  0.6 2.2 %copy-start = (f32[6,16,4,256]{3,2,1,0:T(4,128)S(1)}, f32[6,16,4,256]{3,2,1,0:T(4,128)}, u32[]{:S(2)}) copy-start(f32[6,16,4,256]{3,2,1,0:T(4,128)} %flow.1) | copy-start | bytes 1179652
  1.6 1.2 %copy-start.1 = (f32[8,24,128]{2,1,0:T(8,128)S(1)}, f32[8,24,128]{2,1,0:T(8,128)}, u32[]{:S(2)}) copy-start(f32[8,24,128]{2,1,0:T(8,128)} %rbf.1) | copy-start | bytes 294916
  1.6 1.2 %copy-start.2 = (f32[16,4,256]{2,1,0:T(4,128)S(1)}, f32[16,4,256]{2,1,0:T(4,128)}, u32[]{:S(2)}) copy-start(f32[16,4,256]{2,1,0:T(4,128)} %visc.1) | copy-start | bytes 196612
  1.6 1.2 %copy-start.3 = (s32[8,256]{1,0:T(8,128)S(1)}, s32[8,256]{1,0:T(8,128)}, u32[]{:S(2)}) copy-start(s32[8,256]{1,0:T(8,128)} %kcols.1) | copy-start | bytes 24580
  1.6 1.2 %copy-start.4 = (s32[4,128]{1,0:T(4,128)S(1)}, s32[4,128]{1,0:T(4,128)}, u32[]{:S(2)}) copy-start(s32[4,128]{1,0:T(4,128)} %cols.1) | copy-start | bytes 6148

commit v2 on v1

--- a/solution.py
+++ b/solution.py
@@ -13,6 +13,7 @@
 DOF = 6
 WALL = 3
 CORES = 2
+CG_ITERS = 4
 REACH = 2
 
 
@@ -39,6 +40,33 @@
     return out[:rows] + out[rows : 2 * rows] + out[2 * rows :]
 
 
+def split(x):
+    big = 4097.0 * x
+    high = big - (big - x)
+    return high, x - high
+
+
+def times_exact(one, two, one_parts, two_parts):
+    (one_h, one_l), (two_h, two_l) = one_parts, two_parts
+    high = one * two
+    low = ((one_h * two_h - high) + one_h * two_l + one_l * two_h) + one_l * two_l
+    return high, low
+
+
+def add_pairs(one, two):
+    total = one[0] + two[0]
+    back = total - one[0]
+    error = (one[0] - (total - back)) + (two[0] - back)
+    return total, one[1] + two[1] + error
+
+
+def tree(items):
+    while len(items) > 1:
+        half = len(items) // 2
+        items = [add_pairs(items[i], items[i + half]) for i in range(half)]
+    return items[0]
+
+
 NN_DIMS = ((1,), (0,))
 NT_DIMS = ((1,), (1,))
 
@@ -49,13 +77,14 @@
     out_flow, out_shell, out_motion,
     raw, left, right, q0, q1, q2, rbf_v, kw,
     pick, pack, nodes_out, nodes_in, one_hot, one_hot_t, loads_out, loads_in, lhs,
-    part_out, part_in, force_out, force_in, dots1_a, dots1_b, dots2_a, dots2_b,
-    ans_out, ans_in, vals_out, vals_in, ssem, rsem, lsem,
+    part_out, part_in, force_out, force_in, dots_a, dots_b,
+    ans_out, ans_in, vals_out, vals_in, turn, ssem, rsem, lsem, far_sem,
 ):
     nc = CORES
     ng = ny * nc
     nb = ny * nz * nc
     cap = 128 // nz
+    bits_c, bits_z, bits_cap = (n.bit_length() - 1 for n in (nc, nz, cap))
     b = lax.axis_index("blk")
     f = lax.axis_index("face")
     y = b // (nz * nc)
@@ -106,23 +135,26 @@
         copy.start()
     local_k.start()
 
+    first_z = (1, 2, nz - 2, nz - 1) if nz > 5 else range(1, nz)
     around = [(ob, of) for of in range(nf) for ob in range(-REACH, REACH + 1) if (ob, of) != (0, 0)]
     peers = [near(ob, of) for ob, of in around]
     peers += [along_g(d) for d in range(1, ng)]
-    peers += [along_z(d) for d in range(1, nz)]
+    peers += [along_z(d) for d in first_z]
     barrier = pltpu.get_barrier_semaphore()
     for peer in peers:
         pl.semaphore_signal(barrier, inc=1, device_id=peer, device_id_type=MESH)
 
-    pick[...] = (iota((1024, 128), 1) == (iota((1024, 128), 0) // 256) * 32 + (iota((1024, 128), 0) % 256) // 8).astype(BF16)
-    own = owner[...]
+    at_slot = iota((128, 128), 1) - (iota((128, 128), 0) >> 3)
+    for i in range(8):
+        pick[i * 128 : i * 128 + 128, :] = (at_slot == i * 16).astype(F32).astype(BF16)
+    own = jnp.transpose(jnp.broadcast_to(owner[...], (128, 128)))[:, 0:1]
     members = (own == iota((128, nb if nb > 128 else 128), 1)).astype(F32)
     earlier = (iota((128, 128), 0) > iota((128, 128), 1)).astype(F32)
     ahead = jnp.dot(earlier.astype(BF16), members.astype(BF16), preferred_element_type=F32)
     rank = jnp.sum(ahead * members, axis=1, keepdims=True).astype(jnp.int32)
-    own_c = own % nc
-    own_z = (own // nc) % nz
-    own_g = (own // (nz * nc)) * nc + own_c
+    own_c = own & (nc - 1)
+    own_z = (own >> bits_c) & (nz - 1)
+    own_g = (own >> (bits_c + bits_z)) * nc + own_c
     slot = own_z * cap + rank
     lane = iota((128, 128), 1)
     for d in range(ng):
@@ -133,10 +165,28 @@
     packed_nodes = lax.dot_general(
         named.astype(BF16), pack[...], (NN_DIMS, ((), ())), preferred_element_type=F32
     )
+    local_k.wait()
+    largest = None
+    for r in range(DOF):
+        size = sum(jnp.sum(jnp.abs(kw[REACH, r, e]), axis=0, keepdims=True) for e in range(DOF))
+        largest = size if largest is None else jnp.maximum(largest, size)
+    largest = jnp.broadcast_to(jnp.max(largest, axis=1, keepdims=True), (8, 128))
+    node_rows = iota((8, 128), 0) < 4
     for d in range(ng):
-        nodes_out[d] = packed_nodes[:, d * 128 : (d + 1) * 128]
+        nodes_out[d] = jnp.where(node_rows, packed_nodes[:, d * 128 : (d + 1) * 128], largest)
 
     pl.semaphore_wait(barrier, len(peers))
+
+    def pass_on(step, sem):
+        if nz > 2 * step + 1:
+            for d in (step, -step):
+                pl.semaphore_signal(sem, inc=1, device_id=along_z(d), device_id_type=MESH)
+
+    def heard(step, sem):
+        if nz > 2 * step + 1:
+            pl.semaphore_wait(sem, 2)
+
+    pass_on(2, far_sem.at[0])
     for copy in local_wall:
         copy.wait()
 
@@ -200,7 +250,7 @@
             moved = None
             for d in range(3):
                 for v in range(6):
-                    term = jac[(d * 6 + i) * 6 + v] * diffs[v][d]
+                    term = jac[d, i, v] * diffs[v][d]
                     moved = term if moved is None else moved + term
             result.append(centres[i] - moved + visc_here * spreads[i])
         return result
@@ -211,12 +261,14 @@
 
     for copy in wall_halo:
         copy.wait_recv()
+    heard(2, far_sem.at[0])
+    pass_on(4, far_sem.at[1])
     for k in range(WALL):
         clean(k)
     for k in range(WALL - 1):
         first_sweep(k)
     wall = relax(q1, 0, 256, [0])[0]
-    of_point = iota((8, 256), 1) % 8 == iota((8, 256), 0)
+    of_point = (iota((8, 256), 1) & 7) == iota((8, 256), 0)
     spread_wall = jnp.concatenate(
         [jnp.where(of_point, jnp.broadcast_to(wall[2 + i : 3 + i], (8, 256)), 0.0) for i in range(4)],
         axis=1,
@@ -236,12 +288,6 @@
         loads_out[d] = packed[:, d * 128 : (d + 1) * 128]
     load_copies = [send(loads_out.at[d], loads_in.at[d], along_g(d)) for d in range(1, ng)]
 
-    for copy in local_rest:
-        copy.wait()
-    rest_halo = halo(WALL, nk)
-    local_k.wait()
-    k_copies = [send(kw.at[REACH], kw.at[REACH - o], near(o, 0)) for o in (1, -1, 2, -2)]
-
     nodes_in[0] = nodes_out[0]
     loads_in[0] = loads_out[0]
     for copy in node_copies:
@@ -257,8 +303,8 @@
 
     for copy in load_copies:
         copy.wait_recv()
-    slot_z = iota((nz, 24, 128), 2) // cap
-    dest_z = (iota((nz, 24, 128), 0) + z) % nz
+    slot_z = iota((nz, 24, 128), 2) >> bits_cap
+    dest_z = (iota((nz, 24, 128), 0) + z) & (nz - 1)
     to_dest = slot_z == dest_z
     for d in range(ng):
         for k in range(4):
@@ -266,13 +312,22 @@
             masked = jnp.where(to_dest, jnp.broadcast_to(parts[None], (nz, 24, 128)), 0.0)
             at = (d * 4 + k) * 128
             lhs[:, at : at + 128] = masked.reshape(nz * 24, 128).astype(BF16)
+    heard(4, far_sem.at[1])
     dense = jnp.dot(lhs[...], one_hot[...], preferred_element_type=F32)
+    largest = functools.reduce(jnp.maximum, [nodes_in[d, 4:5, :] for d in range(ng)])
+    largest = jnp.concatenate([largest, largest], axis=1)
     for d in range(nz):
+        part_out[d, 6:7, :] = largest
         part = dense[d * 24 : d * 24 + 24]
-        part_out[d] = part[0:8] + part[8:16] + part[16:24]
+        part_out[d, 0:6, :] = (part[0:8] + part[8:16] + part[16:24])[0:6]
     part_copies = [
-        send(part_out.at[d, 0:6, :], part_in.at[d, 0:6, :], along_z(d)) for d in range(1, nz)
+        send(part_out.at[d, 0:7, :], part_in.at[d, 0:7, :], along_z(d)) for d in range(1, nz)
     ]
+
+    for copy in local_rest:
+        copy.wait()
+    rest_halo = halo(WALL, nk)
+    k_copies = [send(kw.at[REACH], kw.at[REACH - o], near(o, 0)) for o in (1, -1, 2, -2)]
 
     for copy in rest_halo:
         copy.wait_recv()
@@ -292,6 +347,8 @@
     for d in range(1, nz):
         part_copies[d - 1].wait_recv()
         total = total + part_in[d, 0:6, :]
+        largest = jnp.maximum(largest, part_in[d, 6:7, :])
+    scale = 1.0 / largest[:, 0:128]
     force_out[...] = total
     force_copies = {}
     for ob, of in around:
@@ -352,14 +409,17 @@
                 shifted[i].append(jnp.where(whole == 0, joined[i - 1], far))
         for i in range(lo, hi):
             shifted[i].append(vec[i])
+            for j in range(8):
+                turn[i, j] = shifted[i][j]
         out = {}
         for i in range(lo, hi):
             lanes = pl.ds((i % 2) * 128, 128)
+            columns = [turn[i, :, e, :] for e in range(DOF)]
             rows = []
             for r in range(DOF):
                 total = None
-                for j in range(8):
-                    term = kw[i // 2, j, r, :, lanes] * shifted[i][j][0:6]
+                for e in range(DOF):
+                    term = kw[i // 2, r, e, :, lanes] * columns[e]
                     total = term if total is None else total + term
                 rows.append(jnp.sum(total, axis=0, keepdims=True))
             rows.append(empty)
@@ -368,77 +428,102 @@
 
     mid = (2 * REACH, 2 * REACH + 1)
 
-    def dot_row(one, two):
-        return jnp.sum(sum(one[i] * two[i] for i in mid), axis=0, keepdims=True)
-
-    def everywhere(rows, buf_a, buf_b):
-        height = buf_a.shape[1]
-        rows = rows + [jnp.zeros((height - len(rows), 128), F32)]
-        buf_a[0] = jnp.concatenate(rows, axis=0)
-        copies = [send(buf_a.at[0], buf_a.at[d], along_z(d)) for d in range(1, nz)]
-        for copy in copies:
-            copy.wait_recv()
-        buf_b[0] = functools.reduce(jnp.add, [buf_a[d] for d in range(nz)])
-        copies = [send(buf_b.at[0], buf_b.at[d], along_g(d)) for d in range(1, ng)]
-        for copy in copies:
-            copy.wait_recv()
-        total = functools.reduce(jnp.add, [buf_b[d] for d in range(ng)])
-        total = jnp.sum(total, axis=1, keepdims=True)
-        return [total[i : i + 1] for i in range(len(rows) - 1)]
-
-    def mix(scales_and_vecs, lo, hi):
-        out = {}
-        for i in range(lo, hi):
-            total = None
-            for scale, vec in scales_and_vecs:
-                term = vec[i] if scale is None else scale * vec[i]
-                total = term if total is None else total + term
-            out[i] = total
-        return out
-
-    v1 = times_k(v0, 1, 9)
-    v2 = times_k(v1, 2, 8)
-    m0, m1, m2, m3 = everywhere(
-        [dot_row(v0, v0), dot_row(v0, v1), dot_row(v1, v1), dot_row(v1, v2)], dots1_a, dots1_b
-    )
-    alpha0 = m0 / m1
-    rr1 = jnp.maximum(m0 - 2.0 * alpha0 * m1 + alpha0 * alpha0 * m2, 0.0)
-    beta0 = rr1 / m0
-    bend1 = (m1 - 2.0 * alpha0 * m2 + alpha0 * alpha0 * m3) + 2.0 * beta0 * (m1 - alpha0 * m2) + beta0 * beta0 * m1
-    alpha1 = rr1 / bend1
-    r1 = mix([(None, v0), (-alpha0, v1)], 2, 8)
-    d1 = mix([(None, r1), (beta0, v0)], 2, 8)
-    t = mix([(1.0 + beta0, v1), (-alpha0, v2)], 2, 8)
-    x2 = mix([(alpha0, v0), (alpha1, d1)], 4, 6)
-    r2 = mix([(None, r1), (-alpha1, t)], 2, 8)
-    s = times_k(r2, 3, 7)
-    u = times_k(s, 4, 6)
-    w = times_k(t, 4, 6)
-    pairs = [(r2, r2), (r2, s), (r2, t), (d1, t), (s, s), (s, t), (t, t), (s, u), (s, w), (t, w)]
-    rr2, rs, rt, dt, ss, st, tt, su, sw, tw = everywhere(
-        [dot_row(one, two) for one, two in pairs], dots2_a, dots2_b
-    )
-    beta1 = rr2 / rr1
-    bend2 = rs + 2.0 * beta1 * rt + beta1 * beta1 * dt
-    alpha2 = rr2 / bend2
-    along = rs + beta1 * rt
-    square = ss + 2.0 * beta1 * st + beta1 * beta1 * tt
-    rr3 = jnp.maximum(rr2 - 2.0 * alpha2 * along + alpha2 * alpha2 * square, 0.0)
-    beta2 = rr3 / rr2
-    bend3 = (
-        rs
-        - 2.0 * alpha2 * (ss + beta1 * st)
-        + alpha2 * alpha2 * (su + 2.0 * beta1 * sw + beta1 * beta1 * tw)
-        + 2.0 * beta2 * (along - alpha2 * square)
-        + beta2 * beta2 * bend2
-    )
-    alpha3 = rr3 / bend3
-    d2 = mix([(None, r2), (beta1, d1)], 4, 6)
-    w2 = mix([(None, s), (beta1, t)], 4, 6)
-    r3 = mix([(None, r2), (-alpha2, w2)], 4, 6)
-    d3 = mix([(None, r3), (beta2, d2)], 4, 6)
-    x4 = mix([(None, x2), (alpha2, d2), (alpha3, d3)], 4, 6)
-    answer = jnp.concatenate([x4[4], x4[5]], axis=1)
+    basis = [v0]
+    for n in range(CG_ITERS):
+        image = times_k(basis[-1], n + 1, 9 - n)
+        fresh = {}
+        for i in image:
+            turned = 2.0 * (scale * image[i]) - basis[-1][i]
+            fresh[i] = turned if n == 0 else 2.0 * turned - basis[-2][i]
+        basis.append(fresh)
+
+    row_id, lane_id = iota((8, 128), 0), iota((8, 128), 1)
+    pairs = [(i, j) for j in range(CG_ITERS + 1) for i in range(min(j + 1, CG_ITERS))]
+    halves = [{i: split(vec[i]) for i in mid} for vec in basis]
+    tiles = [(jnp.zeros((8, 128), F32), jnp.zeros((8, 128), F32)) for _ in range(2)]
+    for at, (m, n) in enumerate(pairs):
+        one, two = [times_exact(basis[m][i], basis[n][i], halves[m][i], halves[n][i]) for i in mid]
+        both = add_pairs(one, two)
+        for step in (4, 2, 1):
+            both = add_pairs(both, (pltpu.roll(both[0], step, 0), pltpu.roll(both[1], step, 0)))
+        here = row_id == at % 8
+        high, low = tiles[at // 8]
+        tiles[at // 8] = (jnp.where(here, both[0], high), jnp.where(here, both[1], low))
+    for step in (64, 32, 16, 8, 4, 2, 1):
+        tiles = [add_pairs(t, (pltpu.roll(t[0], step, 1), pltpu.roll(t[1], step, 1))) for t in tiles]
+    for part in range(2):
+        line = sum(
+            jnp.sum(jnp.where(lane_id == row_id + 8 * k, tiles[k][part], 0.0), axis=0, keepdims=True)
+            for k in range(2)
+        )
+        dots_a[0, part : part + 1, :] = line
+    copies = [send(dots_a.at[0], dots_a.at[d], along_z(d)) for d in range(1, nz)]
+    for copy in copies:
+        copy.wait_recv()
+    line = tree([(dots_a[d, 0:1, :], dots_a[d, 1:2, :]) for d in range(nz)])
+    for part in range(2):
+        dots_b[0, part : part + 1, :] = line[part]
+    copies = [send(dots_b.at[0], dots_b.at[d], along_g(d)) for d in range(1, ng)]
+    for copy in copies:
+        copy.wait_recv()
+    line = tree([(dots_b[d, 0:1, :], dots_b[d, 1:2, :]) for d in range(ng)])
+    gram = []
+    for j in range(CG_ITERS):
+        spots = None
+        for i in range(CG_ITERS + 1):
+            at = pairs.index((min(i, j), max(i, j)))
+            spot = (row_id == i) & (lane_id == at)
+            spots = spot if spots is None else spots | spot
+        column = []
+        for part in line:
+            picked = jnp.where(spots, jnp.broadcast_to(part, (8, 128)), 0.0)
+            column.append(jnp.broadcast_to(jnp.sum(picked, axis=1, keepdims=True), (8, 128)))
+        gram.append((column[0], column[1], split(column[0])))
+
+    def entry(vec, j):
+        return jnp.broadcast_to(vec[j : j + 1], (8, 128))
+
+    def times_gram(vec, terms):
+        total = None
+        for j in range(terms):
+            by = entry(vec, j)
+            high, low = times_exact(gram[j][0], by, gram[j][2], split(by))
+            term = (high, low + gram[j][1] * by)
+            total = term if total is None else add_pairs(total, term)
+        return total[0] + total[1]
+
+    def inner(one, two):
+        return jnp.broadcast_to(jnp.sum(one * two, axis=0, keepdims=True), (8, 128))
+
+    def ratio(top, bottom):
+        return jnp.where(bottom > 0.0, top / bottom, 0.0)
+
+    def mapped(vec):
+        below = pltpu.roll(vec, 1, 0)
+        below = jnp.where(row_id == 1, 2.0 * below, below)
+        return jnp.where(row_id < 7, 0.5 * vec + 0.25 * (below + pltpu.roll(vec, 7, 0)), 0.0)
+
+    resid = jnp.where(row_id == 0, 1.0, 0.0)
+    course = resid
+    weights = jnp.zeros((8, 128), F32)
+    norm = inner(resid, times_gram(resid, 1))
+    for n in range(CG_ITERS):
+        moved = mapped(course)
+        alpha = ratio(norm, inner(moved, times_gram(course, n + 1)))
+        weights = weights + alpha * course
+        if n < CG_ITERS - 1:
+            resid = resid - alpha * moved
+            fresh_norm = jnp.maximum(inner(resid, times_gram(resid, n + 2)), 0.0)
+            course = resid + ratio(fresh_norm, norm) * course
+            norm = fresh_norm
+    answer = []
+    for i in mid:
+        total = None
+        for n in range(CG_ITERS):
+            term = entry(weights, n) * basis[n][i]
+            total = term if total is None else total + term
+        answer.append(scale * total)
+    answer = jnp.concatenate(answer, axis=1)
     ans_out[...] = answer
     ans_copies = [
         send(ans_out.at[0:6, :], ans_in.at[d, 0:6, :], along_z(d)) for d in range(1, nz)
@@ -454,8 +539,8 @@
             ans_copies[d - 1].wait_recv()
             level.append(stacked_parts(jnp.concatenate([ans_in[d, 0:6, :], zero2], axis=0)))
     wide_x = jnp.concatenate(level, axis=0).astype(BF16)
-    from_z = (z + nz - iota((nz, 8, 256), 0)) % nz
-    from_here = (iota((nz, 8, 256), 2) % 128) // cap == from_z
+    from_z = (z + nz - iota((nz, 8, 256), 0)) & (nz - 1)
+    from_here = (iota((nz, 8, 256), 2) & 127) >> bits_cap == from_z
     for d in range(ng):
         for k in (0, 2):
             at = (d * 4 + k) * 128
@@ -485,7 +570,7 @@
     ny = 4 if nb == 128 else 2
     nz = nb // (ny * CORES)
     ng = ny * CORES
-    count = 8 * 2 + 4 + (ng - 1) * 5 + (nz - 1) * 4 + (5 * nf - 1)
+    count = 8 * 2 + 4 + (ng - 1) * 4 + (nz - 1) * 3 + (5 * nf - 1)
 
     def local(flow, visc, jac, rbf, cols, owner, kmat, kcols):
         nk = visc.shape[0]
@@ -501,7 +586,7 @@
             ((6, nk + 2, 8, 384), F32),
             ((6, nk, 8, 256), F32),
             ((8, 24, 128), F32),
-            ((5, 8, 6, 6, 256), F32),
+            ((5, 6, 6, 8, 256), F32),
             ((1024, 128), BF16),
             ((128, ng * 128), BF16),
             ((ng, 8, 128), F32),
@@ -515,14 +600,13 @@
             ((nz, 8, 256), F32),
             ((6, 256), F32),
             ((nf, 5, 6, 256), F32),
-            ((nz, 8, 128), F32),
-            ((ng, 8, 128), F32),
-            ((nz, 16, 128), F32),
-            ((ng, 16, 128), F32),
+            ((nz, 2, 128), F32),
+            ((ng, 2, 128), F32),
             ((8, 256), F32),
             ((nz, 8, 256), F32),
             ((ng, 32, 128), F32),
             ((ng, 32, 128), F32),
+            ((10, 8, 8, 128), F32),
         ]
         return pl.pallas_call(
             functools.partial(kernel, ny, nz, nf),
@@ -538,11 +622,12 @@
                 pltpu.SemaphoreType.DMA((count,)),
                 pltpu.SemaphoreType.DMA((count,)),
                 pltpu.SemaphoreType.DMA((8,)),
+                pltpu.SemaphoreType.REGULAR((2,)),
             ],
             compiler_params=pltpu.CompilerParams(
-                collective_id=0, has_side_effects=True, vmem_limit_bytes=48 * 1024 * 1024
+                collective_id=0, has_side_effects=True, vmem_limit_bytes=60 * 1024 * 1024
             ),
-        )(flow, visc, jac.reshape(-1), rbf, cols, owner, kmat, kcols)
+        )(flow, visc, jac, rbf, cols, owner.reshape(1, -1), kmat.transpose(1, 2, 0, 3), kcols)
 
     placed = (
         P(None, None, "blk", "face"),

time: 101 us -> 83.5 us (0.83)
  Pallas kernels: 96.3 us -> 79 us
  local copies, waits for them, and re-layouts: 4.06 us -> 3.04 us
    pallas_call x1, Pallas kernels: 96.3 us -> 79 us  [local(): pl.pallas_call(functools.partial(kernel, ny, nz, nf), out_shape=(jax.Shap...]
    unnamed x17 -> x7, local copies, waits for them, and re-layouts: 3.21 us -> 3.04 us
where the time goes in v2:
time: 83.5 us; the launch traced here: 82.7 us
  Pallas kernels  79 us (95%)
  local copies, waits for them, and re-layouts  3.04 us (4%)
    pallas_call x1, Pallas kernels, local(): pl.pallas_call(functools.partial(kernel, ny, nz, nf), out_shape=(jax.Shap...  79 us
    unnamed x7, local copies, waits for them, and re-layouts  3.04 us

profile of v2, /device:TPU:1, one launch (start us, length us, event | category | flops | bytes accessed | tf_op | source)
XLA Modules:
  0.0 82.7 jit_solution(9997457023438822791)
XLA Ops:
  0.6 79.0 %shard_map.103 = (f32[6,16,4,256]{3,2,1,0:T(4,128)}, f32[6,256]{1,0:T(8,128)}, f32[8,128]{1,0:T(8,128)}) custom-call(f32[6,16,4,256]{3,2,1,0:T(4,128)} %flow.1, f32[16,4,256]{2,1,0:T(4,128)} %visc.1, f32[3,6,6]{2,1,0:T(8,128)} %jac.1, f32[8,24,128]{2,1,0:T(8,128)} %rbf.1, s32[4,128]{1,0:T(4,128)} %cols.1, s32[1,128]{1,0:T(1,128)} %bitcast.3, ...), custom_call_target="tpu_custom_call" | custom-call | tf_op jit(solution)/shard_map/pallas_call | solution.py:611
  79.7 0.0 copy-start
  79.7 1.8 %copy.14 = f32[6,16,4,256]{3,2,1,0:T(4,128)} copy(f32[6,16,4,256]{3,2,1,0:T(4,128)} %get-tuple-element.6) | data formatting | bytes 786432
  81.4 0.0 copy-done
  81.4 0.0 copy-start.1
  81.4 0.6 copy.15
  82.0 0.1 copy-done.1
  82.1 0.6 copy.16
Async XLA Ops:
  79.7 1.8 %copy-start = (f32[6,256]{1,0:T(8,128)S(1)}, f32[6,256]{1,0:T(8,128)}, u32[]{:S(2)}) copy-start(f32[6,256]{1,0:T(8,128)} %get-tuple-element.7) | copy-start | bytes 18436
  81.4 0.7 copy-start.1

commit v3 on v2

--- a/solution.py
+++ b/solution.py
@@ -207,6 +207,12 @@
     wall_halo = halo(0, WALL)
     node_copies = [send(nodes_out.at[d], nodes_in.at[d], along_g(d)) for d in range(1, ng)]
 
+    k_copies = [send(kw.at[REACH], kw.at[REACH - o], near(o, 0)) for o in (1, -1)]
+    for o, half in ((2, pl.ds(128, 128)), (-2, pl.ds(0, 128))):
+        k_copies.append(send(kw.at[REACH, :, :, :, half], kw.at[REACH - o, :, :, :, half], near(o, 0)))
+    for copy in local_rest:
+        copy.wait()
+
     row8 = iota((8, 384), 0)
     lane384 = iota((8, 384), 1)
     inside = ((b > 0) | (row8 >= 2)) & ((b < nb - 1) | (row8 < 6))
@@ -263,6 +269,7 @@
         copy.wait_recv()
     heard(2, far_sem.at[0])
     pass_on(4, far_sem.at[1])
+    rest_halo = halo(WALL, nk)
     for k in range(WALL):
         clean(k)
     for k in range(WALL - 1):
@@ -324,11 +331,6 @@
         send(part_out.at[d, 0:7, :], part_in.at[d, 0:7, :], along_z(d)) for d in range(1, nz)
     ]
 
-    for copy in local_rest:
-        copy.wait()
-    rest_halo = halo(WALL, nk)
-    k_copies = [send(kw.at[REACH], kw.at[REACH - o], near(o, 0)) for o in (1, -1, 2, -2)]
-
     for copy in rest_halo:
         copy.wait_recv()
 
@@ -360,15 +362,6 @@
             hit = row == iota((256, 128), 0) + 1
             at = (d * 4 + k) * 128
             one_hot_t[:, at : at + 128] = hit.astype(F32).astype(BF16)
-
-    def second_loop(k, carry):
-        for v, val in enumerate(relax(q1, k, 256, range(6))):
-            q2[v, k] = val
-        return carry
-
-    lax.fori_loop(0, nk, second_loop, 0)
-    flow_copy = pltpu.make_async_copy(q2.at[:, :, 2:6, :], out_flow, lsem.at[6])
-    flow_copy.start()
 
     for copy in force_copies.values():
         copy.wait_recv()
@@ -458,6 +451,16 @@
         )
         dots_a[0, part : part + 1, :] = line
     copies = [send(dots_a.at[0], dots_a.at[d], along_z(d)) for d in range(1, nz)]
+
+    def second_loop(k, carry):
+        for v, val in enumerate(relax(q1, k, 256, range(6))):
+            q2[v, k] = val
+        return carry
+
+    lax.fori_loop(0, nk, second_loop, 0)
+    flow_copy = pltpu.make_async_copy(q2.at[:, :, 2:6, :], out_flow, lsem.at[6])
+    flow_copy.start()
+
     for copy in copies:
         copy.wait_recv()
     line = tree([(dots_a[d, 0:1, :], dots_a[d, 1:2, :]) for d in range(nz)])
@@ -563,6 +566,12 @@
     flow_copy.wait()
     for copy in sent:
         copy.wait_send()
+
+
+def hand_over(flow, shell, motion, out_flow, out_shell, out_motion):
+    out_flow[...] = flow[...]
+    out_shell[...] = shell[...]
+    out_motion[...] = motion[...]
 
 
 def solution(mesh):
@@ -608,7 +617,7 @@
             ((ng, 32, 128), F32),
             ((10, 8, 8, 128), F32),
         ]
-        return pl.pallas_call(
+        results = pl.pallas_call(
             functools.partial(kernel, ny, nz, nf),
             out_shape=(
                 jax.ShapeDtypeStruct(flow.shape, F32),
@@ -628,6 +637,13 @@
                 collective_id=0, has_side_effects=True, vmem_limit_bytes=60 * 1024 * 1024
             ),
         )(flow, visc, jac, rbf, cols, owner.reshape(1, -1), kmat.transpose(1, 2, 0, 3), kcols)
+        return pl.pallas_call(
+            hand_over,
+            out_shape=tuple(jax.ShapeDtypeStruct(r.shape, F32) for r in results),
+            in_specs=[vmem] * 3,
+            out_specs=(vmem,) * 3,
+            compiler_params=pltpu.CompilerParams(vmem_limit_bytes=60 * 1024 * 1024),
+        )(*results)
 
     placed = (
         P(None, None, "blk", "face"),

time: 83.5 us -> 76.1 us (0.911)
  Pallas kernels: 79 us -> 75.2 us
  local copies, waits for them, and re-layouts: 3.04 us -> 0 us
    pallas_call x1, Pallas kernels: 79 us -> 73.4 us  [local(): pl.pallas_call(functools.partial(kernel, ny, nz, nf), out_shape=(jax.Shap...]
    unnamed x7 -> x0, local copies, waits for them, and re-layouts: 3.04 us -> none
    pallas_call x0 -> x1, Pallas kernels: none -> 1.79 us  [local(): pl.pallas_call(hand_over, out_shape=tuple((jax.ShapeDtypeStruct(r.shape,...]
where the time goes in v3:
time: 76.1 us; the launch traced here: 75.8 us
  Pallas kernels  75.2 us (99%)
    pallas_call x1, Pallas kernels, local(): pl.pallas_call(functools.partial(kernel, ny, nz, nf), out_shape=(jax.Shap...  73.4 us
    pallas_call x1, Pallas kernels, local(): pl.pallas_call(hand_over, out_shape=tuple((jax.ShapeDtypeStruct(r.shape,...  1.79 us

profile of v3, /device:TPU:1, one launch (start us, length us, event | category | flops | bytes accessed | tf_op | source)
XLA Modules:
  0.0 75.8 jit_solution(1416912163700787639)
XLA Ops:
  0.6 73.4 %shard_map.103 = (f32[6,16,4,256]{3,2,1,0:T(4,128)}, f32[6,256]{1,0:T(8,128)}, f32[8,128]{1,0:T(8,128)}) custom-call(f32[6,16,4,256]{3,2,1,0:T(4,128)} %flow.1, f32[16,4,256]{2,1,0:T(4,128)} %visc.1, f32[3,6,6]{2,1,0:T(8,128)} %jac.1, f32[8,24,128]{2,1,0:T(8,128)} %rbf.1, s32[4,128]{1,0:T(4,128)} %cols.1, s32[1,128]{1,0:T(1,128)} %bitcast.3, ...), custom_call_target="tpu_custom_call" | custom-call | tf_op jit(solution)/shard_map/pallas_call | solution.py:620
  74.0 1.8 %shard_map.104 = (f32[6,16,4,256]{3,2,1,0:T(4,128)}, f32[6,256]{1,0:T(8,128)}, f32[8,128]{1,0:T(8,128)}) custom-call(f32[6,16,4,256]{3,2,1,0:T(4,128)} %get-tuple-element.6.flow, f32[6,256]{1,0:T(8,128)} %get-tuple-element.7.shell, f32[8,128]{1,0:T(8,128)} %get-tuple-element.8.motion), custom_call_target="tpu_custom_call" | custom-call | tf_op jit(solution)/shard_map/pallas_call | solution.py:640

commit v4 on v3

--- a/solution.py
+++ b/solution.py
@@ -78,7 +78,8 @@
     raw, left, right, q0, q1, q2, rbf_v, kw,
     pick, pack, nodes_out, nodes_in, one_hot, one_hot_t, loads_out, loads_in, lhs,
     part_out, part_in, force_out, force_in, dots_a, dots_b,
-    ans_out, ans_in, vals_out, vals_in, turn, ssem, rsem, lsem, far_sem,
+    ans_out, ans_in, vals_out, vals_in, turn,
+    owner_v, cols_v, jac_s, kcols_s, ssem, rsem, lsem, far_sem,
 ):
     nc = CORES
     ng = ny * nc
@@ -116,24 +117,8 @@
         return copy
 
     sent = []
-
-    local_wall = [
-        pltpu.make_async_copy(flow.at[:, 0:WALL], raw.at[0:6, 0:WALL, 2:6, :], lsem.at[0]),
-        pltpu.make_async_copy(visc.at[0:WALL], raw.at[6, 0:WALL, 2:6, :], lsem.at[1]),
-    ]
     nk = visc.shape[0]
-    local_rest = [
-        pltpu.make_async_copy(flow.at[:, WALL:nk], raw.at[0:6, WALL:nk, 2:6, :], lsem.at[2]),
-        pltpu.make_async_copy(visc.at[WALL:nk], raw.at[6, WALL:nk, 2:6, :], lsem.at[3]),
-    ]
-    local_k = pltpu.make_async_copy(kmat, kw.at[REACH], lsem.at[4])
-    local_rbf = pltpu.make_async_copy(rbf, rbf_v, lsem.at[5])
-    for copy in local_wall:
-        copy.start()
-    local_rbf.start()
-    for copy in local_rest:
-        copy.start()
-    local_k.start()
+    far_first = sorted(range(1, nz), key=lambda d: -min(d, nz - d))
 
     first_z = (1, 2, nz - 2, nz - 1) if nz > 5 else range(1, nz)
     around = [(ob, of) for of in range(nf) for ob in range(-REACH, REACH + 1) if (ob, of) != (0, 0)]
@@ -144,10 +129,34 @@
     for peer in peers:
         pl.semaphore_signal(barrier, inc=1, device_id=peer, device_id_type=MESH)
 
+    local_wall = [
+        pltpu.make_async_copy(flow.at[:, 0:WALL], raw.at[0:6, 0:WALL, 2:6, :], lsem.at[0]),
+        pltpu.make_async_copy(visc.at[0:WALL], raw.at[6, 0:WALL, 2:6, :], lsem.at[1]),
+    ]
+    local_rest = [
+        pltpu.make_async_copy(flow.at[:, WALL:nk], raw.at[0:6, WALL:nk, 2:6, :], lsem.at[2]),
+        pltpu.make_async_copy(visc.at[WALL:nk], raw.at[6, WALL:nk, 2:6, :], lsem.at[3]),
+    ]
+    local_k = pltpu.make_async_copy(kmat, kw.at[REACH], lsem.at[4])
+    local_rbf = pltpu.make_async_copy(rbf, rbf_v, lsem.at[5])
+    small = [
+        pltpu.make_async_copy(owner, owner_v, lsem.at[7]),
+        pltpu.make_async_copy(cols, cols_v, lsem.at[8]),
+        pltpu.make_async_copy(jac, jac_s, lsem.at[9]),
+        pltpu.make_async_copy(kcols, kcols_s, lsem.at[10]),
+    ]
+    for copy in local_wall + small:
+        copy.start()
+    local_rbf.start()
+    for copy in local_rest:
+        copy.start()
+    local_k.start()
+
     at_slot = iota((128, 128), 1) - (iota((128, 128), 0) >> 3)
     for i in range(8):
         pick[i * 128 : i * 128 + 128, :] = (at_slot == i * 16).astype(F32).astype(BF16)
-    own = jnp.transpose(jnp.broadcast_to(owner[...], (128, 128)))[:, 0:1]
+    small[0].wait()
+    own = jnp.transpose(jnp.broadcast_to(owner_v[...], (128, 128)))[:, 0:1]
     members = (own == iota((128, nb if nb > 128 else 128), 1)).astype(F32)
     earlier = (iota((128, 128), 0) > iota((128, 128), 1)).astype(F32)
     ahead = jnp.dot(earlier.astype(BF16), members.astype(BF16), preferred_element_type=F32)
@@ -160,7 +169,8 @@
     for d in range(ng):
         here = (own_g == (g + d) % ng) & (slot == lane)
         pack[:, d * 128 : (d + 1) * 128] = here.astype(F32).astype(BF16)
-    named = (cols[...] + 1).astype(F32)
+    small[1].wait()
+    named = (cols_v[...] + 1).astype(F32)
     named = jnp.concatenate([named, jnp.zeros((4, 128), F32)], axis=0)
     packed_nodes = lax.dot_general(
         named.astype(BF16), pack[...], (NN_DIMS, ((), ())), preferred_element_type=F32
@@ -187,6 +197,8 @@
             pl.semaphore_wait(sem, 2)
 
     pass_on(2, far_sem.at[0])
+    small[2].wait()
+    small[3].wait()
     for copy in local_wall:
         copy.wait()
 
@@ -256,7 +268,7 @@
             moved = None
             for d in range(3):
                 for v in range(6):
-                    term = jac[d, i, v] * diffs[v][d]
+                    term = jac_s[d, i, v] * diffs[v][d]
                     moved = term if moved is None else moved + term
             result.append(centres[i] - moved + visc_here * spreads[i])
         return result
@@ -310,26 +322,30 @@
 
     for copy in load_copies:
         copy.wait_recv()
-    slot_z = iota((nz, 24, 128), 2) >> bits_cap
-    dest_z = (iota((nz, 24, 128), 0) + z) & (nz - 1)
-    to_dest = slot_z == dest_z
-    for d in range(ng):
-        for k in range(4):
-            parts = stacked_parts(loads_in[d, k * 8 : k * 8 + 8, :])
-            masked = jnp.where(to_dest, jnp.broadcast_to(parts[None], (nz, 24, 128)), 0.0)
-            at = (d * 4 + k) * 128
-            lhs[:, at : at + 128] = masked.reshape(nz * 24, 128).astype(BF16)
-    heard(4, far_sem.at[1])
-    dense = jnp.dot(lhs[...], one_hot[...], preferred_element_type=F32)
+    many = nz // 2
+    near_base, far_base = -(nz // 4), many - nz // 4
+    slot_z = iota((many, 24, 128), 2) >> bits_cap
     largest = functools.reduce(jnp.maximum, [nodes_in[d, 4:5, :] for d in range(ng)])
     largest = jnp.concatenate([largest, largest], axis=1)
-    for d in range(nz):
-        part_out[d, 6:7, :] = largest
-        part = dense[d * 24 : d * 24 + 24]
-        part_out[d, 0:6, :] = (part[0:8] + part[8:16] + part[16:24])[0:6]
-    part_copies = [
-        send(part_out.at[d, 0:7, :], part_in.at[d, 0:7, :], along_z(d)) for d in range(1, nz)
-    ]
+    heard(4, far_sem.at[1])
+    part_copies = {}
+    for base in (far_base, near_base):
+        to_dest = slot_z == (iota((many, 24, 128), 0) + (z + base + nz)) & (nz - 1)
+        for d in range(ng):
+            for k in range(4):
+                parts = stacked_parts(loads_in[d, k * 8 : k * 8 + 8, :])
+                masked = jnp.where(to_dest, jnp.broadcast_to(parts[None], (many, 24, 128)), 0.0)
+                at = (d * 4 + k) * 128
+                lhs[:, at : at + 128] = masked.reshape(many * 24, 128).astype(BF16)
+        dense = jnp.dot(lhs[...], one_hot[...], preferred_element_type=F32)
+        group = [(i + base) % nz for i in range(many)]
+        for i, d in enumerate(group):
+            part_out[d, 6:7, :] = largest
+            part = dense[i * 24 : i * 24 + 24]
+            part_out[d, 0:6, :] = (part[0:8] + part[8:16] + part[16:24])[0:6]
+        for d in far_first:
+            if d in group:
+                part_copies[d] = send(part_out.at[d, 0:7, :], part_in.at[d, 0:7, :], along_z(d))
 
     for copy in rest_halo:
         copy.wait_recv()
@@ -347,13 +363,13 @@
 
     total = part_out[0, 0:6, :]
     for d in range(1, nz):
-        part_copies[d - 1].wait_recv()
+        part_copies[d].wait_recv()
         total = total + part_in[d, 0:6, :]
         largest = jnp.maximum(largest, part_in[d, 6:7, :])
     scale = 1.0 / largest[:, 0:128]
     force_out[...] = total
     force_copies = {}
-    for ob, of in around:
+    for ob, of in sorted(around, key=lambda p: -min(p[1], nf - p[1]) * 2 - abs(p[0])):
         force_copies[ob, of] = send(force_out, force_in.at[of, ob + REACH], near(ob, of))
 
     for d in range(ng):
@@ -385,7 +401,7 @@
             start.append(jnp.concatenate([full[:, half * 128 : half * 128 + 128], empty], axis=0))
     v0 = dict(enumerate(start))
 
-    reach = [kcols[j, 0] for j in range(8)]
+    reach = [kcols_s[j, 0] for j in range(8)]
     lane128 = iota((8, 128), 1)
 
     def times_k(vec, lo, hi):
@@ -450,7 +466,7 @@
             for k in range(2)
         )
         dots_a[0, part : part + 1, :] = line
-    copies = [send(dots_a.at[0], dots_a.at[d], along_z(d)) for d in range(1, nz)]
+    copies = [send(dots_a.at[0], dots_a.at[d], along_z(d)) for d in far_first]
 
     def second_loop(k, carry):
         for v, val in enumerate(relax(q1, k, 256, range(6))):
@@ -528,31 +544,39 @@
         answer.append(scale * total)
     answer = jnp.concatenate(answer, axis=1)
     ans_out[...] = answer
-    ans_copies = [
-        send(ans_out.at[0:6, :], ans_in.at[d, 0:6, :], along_z(d)) for d in range(1, nz)
-    ]
+    ans_copies = {
+        d: send(ans_out.at[0:6, :], ans_in.at[d, 0:6, :], along_z(d)) for d in far_first
+    }
+    flow_copy.wait()
+    for copy in sent[:-(nz - 1)]:
+        copy.wait_send()
+    late = len(sent) - (nz - 1)
     out_shell[...] = answer[0:6]
 
-    level = []
     zero2 = jnp.zeros((2, 256), F32)
-    for d in range(nz):
-        if d == 0:
-            level.append(stacked_parts(answer))
-        else:
-            ans_copies[d - 1].wait_recv()
-            level.append(stacked_parts(jnp.concatenate([ans_in[d, 0:6, :], zero2], axis=0)))
-    wide_x = jnp.concatenate(level, axis=0).astype(BF16)
-    from_z = (z + nz - iota((nz, 8, 256), 0)) & (nz - 1)
-    from_here = (iota((nz, 8, 256), 2) & 127) >> bits_cap == from_z
-    for d in range(ng):
-        for k in (0, 2):
-            at = (d * 4 + k) * 128
-            got = jnp.dot(wide_x, one_hot_t[:, at : at + 256], preferred_element_type=F32)
-            got = got.reshape(nz, 3, 8, 256)
-            got = got[:, 0] + got[:, 1] + got[:, 2]
-            got = jnp.sum(jnp.where(from_here, got, 0.0), axis=0)
-            vals_out[d, k * 8 : k * 8 + 8, :] = got[:, 0:128]
-            vals_out[d, k * 8 + 8 : k * 8 + 16, :] = got[:, 128:256]
+    slot_z = (iota((many, 8, 256), 2) & 127) >> bits_cap
+    for base in (near_base, far_base):
+        level = []
+        for i in range(many):
+            d = (i + base) % nz
+            if d == 0:
+                level.append(stacked_parts(answer))
+            else:
+                ans_copies[d].wait_recv()
+                level.append(stacked_parts(jnp.concatenate([ans_in[d, 0:6, :], zero2], axis=0)))
+        wide_x = jnp.concatenate(level, axis=0).astype(BF16)
+        from_here = slot_z == (z + 2 * nz - base - iota((many, 8, 256), 0)) & (nz - 1)
+        for d in range(ng):
+            for k in (0, 2):
+                at = (d * 4 + k) * 128
+                got = jnp.dot(wide_x, one_hot_t[:, at : at + 256], preferred_element_type=F32)
+                got = got.reshape(many, 3, 8, 256)
+                got = got[:, 0] + got[:, 1] + got[:, 2]
+                got = jnp.sum(jnp.where(from_here, got, 0.0), axis=0)
+                for half in range(2):
+                    rows = slice((k + half) * 8, (k + half) * 8 + 8)
+                    here = got[:, half * 128 : half * 128 + 128]
+                    vals_out[d, rows, :] = here if base == near_base else vals_out[d, rows, :] + here
     val_copies = [send(vals_out.at[d], vals_in.at[d], along_g(-d)) for d in range(1, ng)]
     returned = [vals_out[0]]
     for d in range(1, ng):
@@ -563,8 +587,7 @@
     motion = [jnp.sum(rbf_v[p] * values, axis=0, keepdims=True) for p in range(8)]
     out_motion[...] = jnp.concatenate(motion, axis=0)
 
-    flow_copy.wait()
-    for copy in sent:
+    for copy in sent[late:]:
         copy.wait_send()
 
 
@@ -584,7 +607,6 @@
     def local(flow, visc, jac, rbf, cols, owner, kmat, kcols):
         nk = visc.shape[0]
         vmem = pl.BlockSpec(memory_space=pltpu.VMEM)
-        smem = pl.BlockSpec(memory_space=pltpu.SMEM)
         hbm = pl.BlockSpec(memory_space=pl.ANY)
         k_total = ng * 512
         scratch = [
@@ -604,7 +626,7 @@
             ((256, k_total), BF16),
             ((ng, 32, 128), F32),
             ((ng, 32, 128), F32),
-            ((nz * 24, k_total), BF16),
+            ((nz // 2 * 24, k_total), BF16),
             ((nz, 8, 256), F32),
             ((nz, 8, 256), F32),
             ((6, 256), F32),
@@ -624,13 +646,17 @@
                 jax.ShapeDtypeStruct((6, 256), F32),
                 jax.ShapeDtypeStruct((8, 128), F32),
             ),
-            in_specs=[hbm, hbm, smem, hbm, vmem, vmem, hbm, smem],
+            in_specs=[hbm] * 8,
             out_specs=(hbm, vmem, vmem),
             scratch_shapes=[pltpu.VMEM(shape, kind) for shape, kind in scratch]
             + [
+                pltpu.VMEM((1, 128), jnp.int32),
+                pltpu.VMEM((4, 128), jnp.int32),
+                pltpu.SMEM((3, 6, 6), F32),
+                pltpu.SMEM((8, 256), jnp.int32),
                 pltpu.SemaphoreType.DMA((count,)),
                 pltpu.SemaphoreType.DMA((count,)),
-                pltpu.SemaphoreType.DMA((8,)),
+                pltpu.SemaphoreType.DMA((11,)),
                 pltpu.SemaphoreType.REGULAR((2,)),
             ],
             compiler_params=pltpu.CompilerParams(

time: 76.1 us -> 72.2 us (0.949)
  Pallas kernels: 75.2 us -> 71.4 us
    pallas_call x1, Pallas kernels: 73.4 us -> 69.6 us  [local(): pl.pallas_call(functools.partial(kernel, ny, nz, nf), out_shape=(jax.Shap...]
where the time goes in v4:
time: 72.2 us; the launch traced here: 72 us
  Pallas kernels  71.4 us (99%)
    pallas_call x1, Pallas kernels, local(): pl.pallas_call(functools.partial(kernel, ny, nz, nf), out_shape=(jax.Shap...  69.6 us
    pallas_call x1, Pallas kernels, local(): pl.pallas_call(hand_over, out_shape=tuple((jax.ShapeDtypeStruct(r.shape,...  1.79 us

profile of v4, /device:TPU:1, one launch (start us, length us, event | category | flops | bytes accessed | tf_op | source)
XLA Modules:
  0.0 72.0 jit_solution(9629453295912440041)
XLA Ops:
  0.6 69.6 %shard_map.103 = (f32[6,16,4,256]{3,2,1,0:T(4,128)}, f32[6,256]{1,0:T(8,128)}, f32[8,128]{1,0:T(8,128)}) custom-call(f32[6,16,4,256]{3,2,1,0:T(4,128)} %flow.1, f32[16,4,256]{2,1,0:T(4,128)} %visc.1, f32[3,6,6]{2,1,0:T(8,128)} %jac.1, f32[8,24,128]{2,1,0:T(8,128)} %rbf.1, s32[4,128]{1,0:T(4,128)} %cols.1, s32[1,128]{1,0:T(1,128)} %bitcast.3, ...), custom_call_target="tpu_custom_call" | custom-call | tf_op jit(solution)/shard_map/pallas_call | solution.py:642
  70.2 1.8 %shard_map.104 = (f32[6,16,4,256]{3,2,1,0:T(4,128)}, f32[6,256]{1,0:T(8,128)}, f32[8,128]{1,0:T(8,128)}) custom-call(f32[6,16,4,256]{3,2,1,0:T(4,128)} %get-tuple-element.6.flow, f32[6,256]{1,0:T(8,128)} %get-tuple-element.7.shell, f32[8,128]{1,0:T(8,128)} %get-tuple-element.8.motion), custom_call_target="tpu_custom_call" | custom-call | tf_op jit(solution)/shard_map/pallas_call | solution.py:666

commit v5 on v4

--- a/solution.py
+++ b/solution.py
@@ -219,9 +219,6 @@
     wall_halo = halo(0, WALL)
     node_copies = [send(nodes_out.at[d], nodes_in.at[d], along_g(d)) for d in range(1, ng)]
 
-    k_copies = [send(kw.at[REACH], kw.at[REACH - o], near(o, 0)) for o in (1, -1)]
-    for o, half in ((2, pl.ds(128, 128)), (-2, pl.ds(0, 128))):
-        k_copies.append(send(kw.at[REACH, :, :, :, half], kw.at[REACH - o, :, :, :, half], near(o, 0)))
     for copy in local_rest:
         copy.wait()
 
@@ -347,6 +344,9 @@
             if d in group:
                 part_copies[d] = send(part_out.at[d, 0:7, :], part_in.at[d, 0:7, :], along_z(d))
 
+    k_copies = [send(kw.at[REACH], kw.at[REACH - o], near(o, 0)) for o in (1, -1)]
+    for o, half in ((2, pl.ds(128, 128)), (-2, pl.ds(0, 128))):
+        k_copies.append(send(kw.at[REACH, :, :, :, half], kw.at[REACH - o, :, :, :, half], near(o, 0)))
     for copy in rest_halo:
         copy.wait_recv()
 

time: 72.2 us -> 70.9 us (0.982)
  Pallas kernels: 71.4 us -> 70.1 us
    pallas_call x1, Pallas kernels: 69.6 us -> 68.3 us  [local(): pl.pallas_call(functools.partial(kernel, ny, nz, nf), out_shape=(jax.Shap...]
where the time goes in v5:
time: 70.9 us; the launch traced here: 70.7 us
  Pallas kernels  70.1 us (99%)
    pallas_call x1, Pallas kernels, local(): pl.pallas_call(functools.partial(kernel, ny, nz, nf), out_shape=(jax.Shap...  68.3 us
    pallas_call x1, Pallas kernels, local(): pl.pallas_call(hand_over, out_shape=tuple((jax.ShapeDtypeStruct(r.shape,...  1.79 us

profile of v5, /device:TPU:1, one launch (start us, length us, event | category | flops | bytes accessed | tf_op | source)
XLA Modules:
  0.0 70.7 jit_solution(16669537597791099621)
XLA Ops:
  0.6 68.3 %shard_map.103 = (f32[6,16,4,256]{3,2,1,0:T(4,128)}, f32[6,256]{1,0:T(8,128)}, f32[8,128]{1,0:T(8,128)}) custom-call(f32[6,16,4,256]{3,2,1,0:T(4,128)} %flow.1, f32[16,4,256]{2,1,0:T(4,128)} %visc.1, f32[3,6,6]{2,1,0:T(8,128)} %jac.1, f32[8,24,128]{2,1,0:T(8,128)} %rbf.1, s32[4,128]{1,0:T(4,128)} %cols.1, s32[1,128]{1,0:T(1,128)} %bitcast.3, ...), custom_call_target="tpu_custom_call" | custom-call | tf_op jit(solution)/shard_map/pallas_call | solution.py:642
  68.9 1.8 %shard_map.104 = (f32[6,16,4,256]{3,2,1,0:T(4,128)}, f32[6,256]{1,0:T(8,128)}, f32[8,128]{1,0:T(8,128)}) custom-call(f32[6,16,4,256]{3,2,1,0:T(4,128)} %get-tuple-element.6.flow, f32[6,256]{1,0:T(8,128)} %get-tuple-element.7.shell, f32[8,128]{1,0:T(8,128)} %get-tuple-element.8.motion), custom_call_target="tpu_custom_call" | custom-call | tf_op jit(solution)/shard_map/pallas_call | solution.py:666
